TPU v7x, 512 devices: a whole 4x4x16 slice. The times are simulated.
512 devices in a mesh: grp: 32 (over y, x, core), row: 16 (over z).
Axes of the slice: x: 4, y: 4, z: 16, core: 2. Of those that a mesh axis runs over, the one named last changes fastest.
Arguments:
- embedded: bfloat16 [2048, 128, 768], P(('grp', 'row')), may hold values from -0.59765625 to 0.59765625
- cotangent: bfloat16 [2048, 128, 768], P(('grp', 'row')), may hold values from -6 to 6
- w_query: bfloat16 [768, 768], P('row'), may hold values from -1 to 1
- w_key: bfloat16 [768, 768], P('row'), may hold values from -1 to 1
- w_value: bfloat16 [768, 768], P('row'), may hold values from -0.21875 to 0.21875
- w_output: bfloat16 [768, 768], P('row'), may hold values from -0.21875 to 0.21875
- helpers: int32 [32], replicated, may hold values from 0 to 31, as said below
- helped_row_flag: int32 [2048], P(('grp', 'row')), may hold values from 0 to 1, as said below
- row_live: int32 [2048], P(('grp', 'row')), may hold values from 0 to 1, as said below
Outputs:
- layer_out: bfloat16 [2048, 128, 768], P(('grp', 'row'))
- grad_in: bfloat16 [2048, 128, 768], P(('grp', 'row'))
Inputs may be any that keep to these rules, and one draw needn't show every extreme that they name: helpers names for each group the one MSA whose extra rows it may hold; it may name the group itself. `helped_row_flag`: the first slot of every device holds a row of its group's own MSA. `row_live`: the first slot of every device is live.
All inputs are finite; a program needn't handle non-finite values.
Results may differ from a plain program's by a relative error of at most 0.0085.
The roundings to bfloat16 on the way count: a program that leaves them out, or rounds other values in their place, can miss the bound.
Values may be sent and summed in bfloat16 or wider, within the bound.
A program may use at most 64 MiB of HBM per device.

v0:
```python
import math

import jax
import jax.numpy as jnp
from jax import lax
from jax.sharding import PartitionSpec as P

HEADS = 12


def layer_norm(rows_in):
    center = jnp.mean(rows_in, axis=-1, keepdims=True)
    centred = rows_in - center
    spread = jnp.mean(centred * centred, axis=-1, keepdims=True)
    return centred * lax.rsqrt(spread + 1e-05)


def times_transpose(left, weight):
    return lax.dot_general(
        left, weight, (((1,), (1,)), ((), ())), preferred_element_type=jnp.float32
    )


def pair_terms(left, right, first, second):
    one = jnp.einsum(
        "rihd,rjhd->hij",
        left * first[:, None, None, None],
        right,
        preferred_element_type=jnp.float32,
    )
    two = jnp.einsum(
        "rihd,rjhd->hij",
        left * second[:, None, None, None],
        right,
        preferred_element_type=jnp.float32,
    )
    return jnp.stack([one, two])


def select_sum(helped, gathered):
    shape_one = (helped.shape[0],) + (1,) * (gathered.ndim - 1)
    return jnp.sum(gathered * helped.reshape(shape_one), axis=0)


def normalise(scores, depths, head_size):
    scaling = 1.0 / (math.sqrt(head_size) * jnp.sqrt(depths))
    return (jax.nn.softmax(scores * scaling, axis=-1), scaling)


def score_grads(attend, grads, scaling):
    return (attend * (grads - jnp.sum(grads * attend, axis=-1, keepdims=True)) * scaling).astype(
        jnp.bfloat16
    )


def per_device(
    embedded, cotangent, w_query, w_key, w_value, w_output, helpers, helped_row_flag, row_live
):
    w_query, w_key, w_value, w_output = (
        lax.all_gather(w_query, "row", axis=0, tiled=True),
        lax.all_gather(w_key, "row", axis=0, tiled=True),
        lax.all_gather(w_value, "row", axis=0, tiled=True),
        lax.all_gather(w_output, "row", axis=0, tiled=True),
    )
    local_rows, length, model_width = embedded.shape
    head_size = model_width // HEADS
    head_shape = (local_rows, length, HEADS, head_size)
    flat_shape = (local_rows * length, model_width)
    my_group = lax.axis_index("grp")
    row_devices = lax.axis_size("row")
    flat_in = embedded.astype(jnp.float32).reshape(flat_shape)
    normed_f, norm_back = jax.vjp(layer_norm, flat_in)
    normed = normed_f.astype(jnp.bfloat16)
    queries = (
        jnp.dot(normed, w_query, preferred_element_type=jnp.float32)
        .astype(jnp.bfloat16)
        .reshape(head_shape)
    )
    key_rows = (
        jnp.dot(normed, w_key, preferred_element_type=jnp.float32)
        .astype(jnp.bfloat16)
        .reshape(head_shape)
    )
    values = (
        jnp.dot(normed, w_value, preferred_element_type=jnp.float32)
        .astype(jnp.bfloat16)
        .reshape(head_shape)
    )
    flat_cot = cotangent.reshape(flat_shape)
    dattend = times_transpose(flat_cot, w_output).astype(jnp.bfloat16).reshape(head_shape)
    target = helpers[my_group]
    is_home = (helped_row_flag == 0) | (target == my_group)
    live_rows = row_live.astype(jnp.float32)
    home_live = jnp.where(is_home, live_rows, 0.0)
    help_live = jnp.where(is_home, 0.0, live_rows)
    home_flag = is_home.astype(jnp.float32)
    help_flag = 1.0 - home_flag
    tallies = jnp.stack(
        [jnp.full((row_devices,), jnp.sum(home_live)), jnp.full((row_devices,), jnp.sum(help_live))]
    )
    helped = (helpers == my_group).astype(jnp.float32)
    scores_part = pair_terms(
        queries, key_rows, home_live.astype(jnp.bfloat16), help_live.astype(jnp.bfloat16)
    )
    summed, counted = (
        lax.psum_scatter(scores_part, "row", scatter_dimension=2, tiled=True),
        lax.psum_scatter(tallies, "row", scatter_dimension=1, tiled=True),
    )
    outer, outer_count = (
        lax.all_gather(summed[1][None], "grp", axis=0, tiled=True),
        lax.all_gather(counted[1], "grp", axis=0, tiled=True),
    )
    depths = counted[0, 0] + jnp.sum(helped * outer_count)
    attend, scaling = normalise(summed[0] + select_sum(helped, outer), depths, head_size)
    attend_b = attend.astype(jnp.bfloat16)
    far_probs = lax.all_gather(attend_b[None], "grp", axis=0, tiled=True)
    their_probs = lax.dynamic_index_in_dim(far_probs, target, 0, keepdims=False)
    probs_home, probs_help = (
        lax.all_gather(attend_b, "row", axis=1, tiled=True),
        lax.all_gather(their_probs, "row", axis=1, tiled=True),
    )
    grads_part = pair_terms(
        dattend, values, home_flag.astype(jnp.bfloat16), help_flag.astype(jnp.bfloat16)
    )
    grad_summed = lax.psum_scatter(grads_part, "row", scatter_dimension=2, tiled=True)
    grad_outer = lax.all_gather(grad_summed[1][None], "grp", axis=0, tiled=True)
    dlogit = score_grads(attend, grad_summed[0] + select_sum(helped, grad_outer), scaling)
    far_dlog = lax.all_gather(dlogit[None], "grp", axis=0, tiled=True)
    their_dlog = lax.dynamic_index_in_dim(far_dlog, target, 0, keepdims=False)
    dlog_home, dlog_help = (
        lax.all_gather(dlogit, "row", axis=1, tiled=True),
        lax.all_gather(their_dlog, "row", axis=1, tiled=True),
    )
    home_rows = is_home[:, None, None, None]
    row_probs = jnp.where(home_rows, probs_home[None], probs_help[None])
    row_dlog = jnp.where(home_rows, dlog_home[None], dlog_help[None])
    attended = jnp.einsum(
        "rhij,rjhd->rihd", row_probs, values, preferred_element_type=jnp.float32
    ).astype(jnp.bfloat16)
    layer_out = (
        (
            flat_in
            + jnp.dot(attended.reshape(flat_shape), w_output, preferred_element_type=jnp.float32)
        )
        .astype(jnp.bfloat16)
        .reshape(embedded.shape)
    )
    live_four = live_rows[:, None, None, None]
    dvalue = jnp.einsum(
        "rhij,rihd->rjhd", row_probs, dattend, preferred_element_type=jnp.float32
    ).astype(jnp.bfloat16)
    dquery = (
        jnp.einsum("rhij,rjhd->rihd", row_dlog, key_rows, preferred_element_type=jnp.float32)
        * live_four
    ).astype(jnp.bfloat16)
    dkey = (
        jnp.einsum("rhij,rihd->rjhd", row_dlog, queries, preferred_element_type=jnp.float32)
        * live_four
    ).astype(jnp.bfloat16)
    dnormed = (
        times_transpose(dquery.reshape(flat_shape), w_query)
        + times_transpose(dkey.reshape(flat_shape), w_key)
        + times_transpose(dvalue.reshape(flat_shape), w_value)
    )
    grad_in = (
        (flat_cot.astype(jnp.float32) + norm_back(dnormed)[0])
        .astype(jnp.bfloat16)
        .reshape(embedded.shape)
    )
    return (layer_out, grad_in)


def solution(mesh):
    placed = (
        P(("grp", "row"), None, None),
        P(("grp", "row"), None, None),
        P("row", None),
        P("row", None),
        P("row", None),
        P("row", None),
        P(),
        P(("grp", "row")),
        P(("grp", "row")),
    )
    return jax.shard_map(
        per_device,
        mesh=mesh,
        in_specs=placed,
        out_specs=(P(("grp", "row"), None, None), P(("grp", "row"), None, None)),
        check_vma=False,
    )
```

profile of v0, /device:TPU:6, one launch (start us, length us, event | category | flops | bytes accessed | tf_op | source)
XLA Modules:
  0.0 755.2 jit_solution(12806762867421695777)
XLA Ops:
  15.8 70.3 %all-gather.10.cloned.1.call-done = bf16[768,768]{1,0:T(8,128)(2,1)} async-done(((bf16[48,768]{1,0:T(8,128)(2,1)}), bf16[768,768]{1,0:T(8,128)(2,1)}) %all-gather.10.cloned.1.call-update) | async-done | bytes 1179664 | tf_op jit(solution)/shard_map/all_gather | solution.py:62
  86.0 2.0 convolution_convert_fusion.3
  88.6 68.0 %all-gather.18.cloned.1.call-done = bf16[768,768]{1,0:T(8,128)(2,1)} async-done(((bf16[48,768]{1,0:T(8,128)(2,1)}), bf16[768,768]{1,0:T(8,128)(2,1)}) %all-gather.18.cloned.1.call-update) | async-done | bytes 1179664 | tf_op jit(solution)/shard_map/all_gather | solution.py:63
  156.6 2.1 convolution_convert_fusion
  162.0 65.1 %all-gather.14.cloned.1.call-done = bf16[768,768]{1,0:T(8,128)(2,1)} async-done(((bf16[48,768]{1,0:T(8,128)(2,1)}), bf16[768,768]{1,0:T(8,128)(2,1)}) %all-gather.14.cloned.1.call-update) | async-done | bytes 1179664 | tf_op jit(solution)/shard_map/all_gather | solution.py:61
  227.2 2.9 convolution_convert_fusion.1
  232.6 65.0 %all-gather.12.cloned.1.call-done = bf16[768,768]{1,0:T(8,128)(2,1)} async-done(((bf16[48,768]{1,0:T(8,128)(2,1)}), bf16[768,768]{1,0:T(8,128)(2,1)}) %all-gather.12.cloned.1.call-update) | async-done | bytes 1179664 | tf_op jit(solution)/shard_map/all_gather | solution.py:60
  297.6 2.0 convolution_convert_fusion.2
  303.4 65.4 %reduce-scatter.6.cloned.1.call-done = f32[2,12,8,128]{3,2,1,0:T(8,128)} async-done(((f32[2,12,128,128]{3,2,1,0:T(8,128)}), f32[2,12,8,128]{3,2,1,0:T(8,128)}) %reduce-scatter.6.cloned.1.call-update) | async-done | bytes 98320 | tf_op jit(solution)/shard_map/reduce_scatter | solution.py:125
  368.9 1.4 slice.27
  370.4 70.9 %reduce-scatter.4.cloned.1.call-done = f32[2,12,8,128]{3,2,1,0:T(8,128)} async-done(((f32[2,12,128,128]{3,2,1,0:T(8,128)}), f32[2,12,8,128]{3,2,1,0:T(8,128)}) %reduce-scatter.4.cloned.1.call-update) | async-done | bytes 98320 | tf_op jit(solution)/shard_map/reduce_scatter | solution.py:106
  441.2 1.4 slice.25
  447.6 28.6 %all-reduce.2 = f32[2,16]{1,0:T(2,128)S(1)} all-reduce(f32[2,16]{1,0:T(2,128)S(1)} %stack.27), channel_id=6, replica_groups=mesh['grp'=32,'row'=16] {'row'}, use_global_device_ids=true, to_apply=%region_6.7.clone | all-reduce | flops 32 | bytes 256
  478.5 49.4 %all-reduce.1 = f32[32]{0:T(128)S(1)} all-reduce(f32[32]{0:T(128)S(1)} %bitcast_dynamic-update-slice_fusion), channel_id=2, replica_groups=mesh['grp'=32,'row'=16] {'grp'}, use_global_device_ids=true, to_apply=%add.1 | all-reduce | flops 32 | bytes 256 | tf_op jit(solution)/shard_map/all_gather | solution.py:111
  530.4 31.8 %all-gather.16.cloned.1.call-done = f32[32,12,8,128]{3,2,1,0:T(8,128)} async-done(((f32[1,12,8,128]{3,2,1,0:T(8,128)}), f32[32,12,8,128]{3,2,1,0:T(8,128)}) %all-gather.16.cloned.1.call-update) | async-done | bytes 1572880 | tf_op jit(solution)/shard_map/all_gather | solution.py:110
  562.1 2.2 multiply_reduce_fusion
  564.9 32.6 %all_gather.49 = bf16[12,128,128]{2,1,0:T(8,128)(2,1)S(1)} all-gather(bf16[12,8,128]{2,1,0:T(8,128)(2,1)S(1)} %get-tuple-element.15), channel_id=1, replica_groups=mesh['grp'=32,'row'=16] {'row'}, dimensions={1}, use_global_device_ids=true | all-gather | bytes 417792 | tf_op jit(solution)/shard_map/all_gather | solution.py:131
  597.6 22.9 %all_gather.50 = bf16[32,12,8,128]{3,2,1,0:T(8,128)(2,1)S(1)} all-gather(bf16[1,12,8,128]{3,2,1,0:T(8,128)(2,1)S(1)} %get-tuple-element.13), channel_id=1, replica_groups=mesh['grp'=32,'row'=16] {'grp'}, dimensions={0}, use_global_device_ids=true | all-gather | bytes 811008 | tf_op jit(solution)/shard_map/all_gather | solution.py:128
  620.5 29.6 %all-gather.2 = bf16[1,12,128,128]{3,2,1,0:T(8,128)(2,1)S(1)} all-gather(bf16[1,12,8,128]{3,2,1,0:T(8,128)(2,1)S(1)} %constant_dynamic-slice_fusion.1), channel_id=4, replica_groups=mesh['grp'=32,'row'=16] {'row'}, dimensions={2}, use_global_device_ids=true | all-gather | bytes 417792 | tf_op jit(solution)/shard_map/all_gather | solution.py:132
  652.1 29.8 %all_gather.44 = bf16[12,128,128]{2,1,0:T(8,128)(2,1)S(1)} all-gather(bf16[12,8,128]{2,1,0:T(8,128)(2,1)S(1)} %get-tuple-element.16), channel_id=1, replica_groups=mesh['grp'=32,'row'=16] {'row'}, dimensions={1}, use_global_device_ids=true | all-gather | bytes 417792 | tf_op jit(solution)/shard_map/all_gather | solution.py:119
  681.9 24.1 %all_gather.45 = bf16[32,12,8,128]{3,2,1,0:T(8,128)(2,1)S(1)} all-gather(bf16[1,12,8,128]{3,2,1,0:T(8,128)(2,1)S(1)} %get-tuple-element.14), channel_id=1, replica_groups=mesh['grp'=32,'row'=16] {'grp'}, dimensions={0}, use_global_device_ids=true | all-gather | bytes 811008 | tf_op jit(solution)/shard_map/all_gather | solution.py:116
  706.0 29.4 %all-gather.1 = bf16[1,12,128,128]{3,2,1,0:T(8,128)(2,1)S(1)} all-gather(bf16[1,12,8,128]{3,2,1,0:T(8,128)(2,1)S(1)} %constant_dynamic-slice_fusion.2), channel_id=3, replica_groups=mesh['grp'=32,'row'=16] {'row'}, dimensions={2}, use_global_device_ids=true | all-gather | bytes 417792 | tf_op jit(solution)/shard_map/all_gather | solution.py:120
  745.2 1.5 add_convert_fusion
  746.7 1.7 fusion.15
  (106 shorter events, 37.0 us)
Async XLA Ops:
  7.2 7.9 %copy-start = (bf16[4,128,768]{2,1,0:T(8,128)(2,1)S(1)}, bf16[4,128,768]{2,1,0:T(8,128)(2,1)}, u32[]{:S(2)}) copy-start(bf16[4,128,768]{2,1,0:T(8,128)(2,1)} %param.9) | copy-start | bytes 2359300
  7.2 78.8 %all-gather.10.cloned.1.call-start = ((), (), s32[]{:S(2)}) async-start(), calls=%async_computation.2 | async-start | bytes 1253376 | tf_op jit(solution)/shard_map/all_gather | solution.py:62
  7.9 148.7 %all-gather.18.cloned.1.call-start = ((), (), s32[]{:S(2)}) async-start(), calls=%async_computation.7 | async-start | bytes 1253376 | tf_op jit(solution)/shard_map/all_gather | solution.py:63
  8.7 218.5 %all-gather.14.cloned.1.call-start = ((), (), s32[]{:S(2)}) async-start(), calls=%async_computation.4 | async-start | bytes 1253376 | tf_op jit(solution)/shard_map/all_gather | solution.py:61
  9.4 288.2 %all-gather.12.cloned.1.call-start = ((), (), s32[]{:S(2)}) async-start(), calls=%async_computation.3 | async-start | bytes 1253376 | tf_op jit(solution)/shard_map/all_gather | solution.py:60
  10.0 358.9 %reduce-scatter.6.cloned.1.call-start = ((), (), s32[]{:S(2)}) async-start(), calls=%async_computation.8 | async-start | bytes 1671168 | tf_op jit(solution)/shard_map/reduce_scatter | solution.py:125
  15.8 70.3 %copy-start.5 = (bf16[512,768]{1,0:T(8,128)(2,1)}, bf16[512,768]{1,0:T(8,128)(2,1)S(1)}, u32[]{:S(2)}) copy-start(bf16[512,768]{1,0:T(8,128)(2,1)S(1)} %fusion.11) | copy-start | bytes 2359300
  88.4 68.2 %copy-start.7 = (bf16[4,128,768]{2,1,0:T(8,128)(2,1)S(1)}, bf16[4,128,768]{2,1,0:T(8,128)(2,1)}, u32[]{:S(2)}) copy-start(bf16[4,128,768]{2,1,0:T(8,128)(2,1)} %param.10) | copy-start | bytes 2359300
  88.6 71.7 %copy-start.2 = (bf16[4,128,12,64]{1,0,3,2:T(4,128)(2,1)}, bf16[4,128,12,64]{1,0,3,2:T(4,128)(2,1)S(1)}, u32[]{:S(2)}) copy-start(bf16[4,128,12,64]{1,0,3,2:T(4,128)(2,1)S(1)} %reshape.104) | copy-start | bytes 2359300
  161.9 65.2 %copy-start.6 = (bf16[512,768]{1,0:T(8,128)(2,1)S(1)}, bf16[512,768]{1,0:T(8,128)(2,1)}, u32[]{:S(2)}) copy-start(bf16[512,768]{1,0:T(8,128)(2,1)} %copy-done.5) | copy-start | bytes 2359300
  162.0 279.3 %reduce-scatter.4.cloned.1.call-start = ((), (), s32[]{:S(2)}) async-start(), calls=%async_computation.5 | async-start | bytes 1671168 | tf_op jit(solution)/shard_map/reduce_scatter | solution.py:106
  300.1 1.1 copy-start.4
  303.3 140.5 %copy-start.11 = (s32[4]{0:T(128)S(1)}, s32[4]{0:T(128)}, u32[]{:S(2)}) copy-start(s32[4]{0:T(128)} %param.17) | copy-start | bytes 52
  303.3 224.6 %copy-start.12 = (s32[32]{0:T(128)S(1)}, s32[32]{0:T(128)}, u32[]{:S(2)}) copy-start(s32[32]{0:T(128)} %param.15) | copy-start | bytes 388
  303.4 227.0 %all-gather.20.cloned.1.call-start = ((), (), s32[]{:S(2)}) async-start(), calls=%async_computation.9 | async-start | bytes 1622016 | tf_op jit(solution)/shard_map/all_gather | solution.py:126
  370.3 191.8 %all-gather.16.cloned.1.call-start = ((), (), s32[]{:S(2)}) async-start(), calls=%async_computation.6 | async-start | bytes 1622016 | tf_op jit(solution)/shard_map/all_gather | solution.py:110
  530.3 34.0 %copy-start.10 = (f32[2,12,8,128]{3,2,1,0:T(8,128)S(1)}, f32[2,12,8,128]{3,2,1,0:T(8,128)}, u32[]{:S(2)}) copy-start(f32[2,12,8,128]{3,2,1,0:T(8,128)} %reduce-scatter.4.cloned.1.call-done) | copy-start | bytes 294916
  530.3 34.3 %copy-start.9 = (f32[2,12,8,128]{3,2,1,0:T(8,128)S(1)}, f32[2,12,8,128]{3,2,1,0:T(8,128)}, u32[]{:S(2)}) copy-start(f32[2,12,8,128]{3,2,1,0:T(8,128)} %reduce-scatter.6.cloned.1.call-done) | copy-start | bytes 294916
  735.4 1.1 copy-start.3
  739.1 1.3 copy-start.15
  740.3 1.3 copy-start.14
  741.6 1.3 copy-start.1
  744.0 1.1 copy-start.8
  745.2 1.5 copy-start.13
Sparse Core Ops, SparseCore 0:
  10.1 75.8 all-gather.9
  88.1 68.4 all-gather.17
  158.7 68.4 all-gather.13
  229.1 68.4 all-gather.11
  300.2 68.5 reduce-scatter.5
  371.8 69.4 reduce-scatter.3
  444.9 56.0 all-gather.19
  504.1 57.9 all-gather.15
where the time goes:
time: 756 us; the launch traced here: 755 us
  waiting for transfers between devices  439 us (58%)
  blocking collectives  246 us (33%)
  matrix products  19.3 us (3%)
  local copies, waits for them, and re-layouts  18.8 us (2%)
  between operations  18 us (2%)
  other arithmetic  13.2 us (2%)
    reduce_scatter x1, waiting for transfers between devices, per_device(): lax.psum_scatter(scores_part, 'row', scatter_dimension=2, tiled=True)  70.9 us
    all_gather x1, waiting for transfers between devices, per_device(): lax.all_gather(w_value, 'row', axis=0, tiled=True)  70.3 us
    all_gather x1, waiting for transfers between devices, per_device(): lax.all_gather(w_output, 'row', axis=0, tiled=True)  68 us
    reduce_scatter x1, waiting for transfers between devices, per_device(): lax.psum_scatter(grads_part, 'row', scatter_dimension=2, tiled=True)  65.4 us
    all_gather x1, waiting for transfers between devices, per_device(): lax.all_gather(w_key, 'row', axis=0, tiled=True)  65.1 us
    all_gather x1, waiting for transfers between devices, per_device(): lax.all_gather(w_query, 'row', axis=0, tiled=True)  65 us
    all_gather x1, blocking collectives, per_device(): lax.all_gather(counted[1], 'grp', axis=0, tiled=True)  49.4 us
    all_gather x1, blocking collectives, per_device(): lax.all_gather(dlogit, 'row', axis=1, tiled=True)  32.6 us
  transfers between devices with their start and end apart: 8, of which 7 were waited for; matrix products, arithmetic and copies ran while one was open for 4% of the time, Pallas kernels for 0%

commit v1 on v0

v1 whole, which is shorter than its diff:
```python
import functools

import jax
import jax.numpy as jnp
from jax import lax
from jax.experimental import pallas as pl
from jax.experimental.pallas import tpu as pltpu
from jax.sharding import PartitionSpec as P

HEADS = 12
RDEV = 4
L = 128
D = 768
ZN = 16
SH = D // ZN
QC = D // 2
CH = HEADS * L // ZN
CS = 2 * CH + 8
CG = 2 * CH
PAIRS = HEADS // 2
MESH = pl.DeviceIdType.MESH
F32 = jnp.float32
BF16 = jnp.bfloat16
N_SEM = 256


def rem(a, n):
    return lax.rem(a + n, n)


def dot(a, b):
    return lax.dot_general(a, b, (((1,), (0,)), ((), ())), preferred_element_type=F32)


def dot_t(a, b):
    return lax.dot_general(a, b, (((1,), (1,)), ((), ())), preferred_element_type=F32)


def kernel(
    emb_in,
    cot_in,
    w_query,
    w_key,
    w_value,
    w_output,
    helpers,
    flag,
    live,
    out_ref,
    gin_ref,
    emb,
    cot,
    out,
    gin,
    weights,
    normed,
    queries,
    keys,
    values,
    dattend,
    s_part,
    g_part,
    s_chain,
    g_chain,
    s_plane,
    g_plane,
    s_cross,
    g_cross,
    s_tot,
    g_tot,
    attend,
    probs,
    dlog,
    attended,
    dquery,
    dkey,
    dvalue,
    dnormed,
    send_sems,
    recv_sems,
    own_sems,
):
    g = lax.axis_index("grp")
    z = lax.axis_index("row")
    core = lax.rem(g, 2)
    x = lax.rem(lax.div(g, 2), 4)
    y = lax.div(g, 8)
    sib = g + 1 - 2 * core

    def at(group, row):
        return {"grp": group, "row": row}

    def chip(dx, dy):
        return at((rem(y + dy, 4) * 4 + rem(x + dx, 4)) * 2 + core, z)

    hops = {d: at(g, rem(z + d, ZN)) for d in (5, -5, 1, -1, 2, -2, 3, -3)}
    up, down = hops[1], hops[-1]
    around = {
        (dx, dy): chip(dx, dy) for dx in (1, -1, 0) for dy in (1, -1, 0) if dx != 0 or dy != 0
    }
    other = at(sib, z)
    x_step = 1 - 2 * lax.rem(x + core, 2)
    y_step = 1 - 2 * lax.rem(y + core, 2)
    partners = (chip(x_step, 0), chip(0, y_step), chip(x_step, y_step))

    barrier = pltpu.get_barrier_semaphore()
    peers = [*hops.values(), *around.values(), other]
    for peer in peers:
        pl.semaphore_signal(barrier, inc=1, device_id=peer, device_id_type=MESH)

    started = []
    used = [0]

    def take(count):
        used[0] += count
        assert used[0] <= N_SEM
        return used[0] - count

    def send(src, dst, peer):
        index = take(1)
        copy = pltpu.make_async_remote_copy(
            src_ref=src,
            dst_ref=dst,
            send_sem=send_sems.at[index],
            recv_sem=recv_sems.at[index],
            device_id=peer,
            device_id_type=MESH,
        )
        copy.start()
        started.append(copy)
        return copy

    def wait(copies):
        for copy in copies:
            copy.wait_recv()

    own_rows = pl.ds(pl.multiple_of(z * SH, 16), SH)
    shards = [
        pltpu.make_async_copy(ref, weights.at[m, own_rows, :], own_sems.at[m])
        for m, ref in enumerate((w_query, w_key, w_value, w_output))
    ]
    get_emb = pltpu.make_async_copy(emb_in, emb, own_sems.at[4])
    get_cot = pltpu.make_async_copy(cot_in, cot, own_sems.at[5])
    for copy in (*shards, get_emb, get_cot):
        copy.start()
    for copy in shards:
        copy.wait()

    pl.semaphore_wait(barrier, len(peers))

    def w_piece(shard):
        return weights.at[
            2 * core + lax.rem(y, 2),
            pl.ds(pl.multiple_of(shard * SH, 16), SH),
            pl.ds(pl.multiple_of(lax.rem(x, 2) * QC, 128), QC),
        ]

    def w_rows(shard):
        return weights.at[pl.ds(2 * core, 2), pl.ds(pl.multiple_of(shard * SH, 16), SH), :]

    class Spread:
        def __init__(self, piece):
            self.piece = piece
            self.arriving = {}
            for hop in (5, -5, 1, -1, 2, -2):
                self.send(0, hop)

        def send(self, d, hop):
            ref = self.piece(d)
            self.arriving[d - hop] = send(ref, ref, hops[hop])

        def second(self):
            self.wait(5, -5)
            self.send(5, -3)
            for hop in (2, -2, 1, -1):
                for d in (5, -5):
                    self.send(d, hop)

        def wait(self, *which):
            for d in which:
                self.arriving[d].wait_recv()

    def weight_relay():
        in_a, in_s = {}, []

        def along(*dists):
            for d in dists:
                ref = w_piece(rem(z + d, ZN))
                in_a[d] = [send(ref, ref, peer) for peer in partners]

        def across(*dists):
            for d in dists:
                wait(in_a[d])
                ref = w_rows(rem(z + d, ZN))
                in_s.append(send(ref, ref, other))

        spread = Spread(lambda d: w_piece(rem(z + d, ZN)))
        yield
        for d in (1, -1, 2, -2):
            spread.wait(d)
            along(d)
        spread.second()
        along(5, -5)
        across(1, -1, 2, -2)
        across(5, -5)
        for d in (7, -7, 3, -3, 6, -6, 4, -4, 8):
            spread.wait(d)
            along(d)
        across(7, -7, 3, -3, 6, -6, 4, -4, 8)
        wait(in_s)

    def chain_sum(part, chain, total, counts):
        kind = chain.dtype
        if counts is None:
            streams = (pl.ds(0, CG),)
        else:
            streams = (pl.ds(0, CH), pl.ds(CH, CS - CH))

        def term(half, chunk):
            rows = pl.ds(pl.multiple_of(chunk * CH, 8), CH)
            if counts is None:
                return jnp.concatenate([part[0, rows, :], part[1, rows, :]], axis=0)
            if half == 1:
                return jnp.concatenate([part[1, rows, :], counts], axis=0)
            return part[0, rows, :]

        def chunk_of(way, s):
            return rem(z + 8 - s, ZN) if way == 0 else rem(z - 7 + s, ZN)

        last = (7, 6)
        flying = {}
        for s in range(9):
            for half in range(len(streams)):
                for way in range(2):
                    if s > last[way] + 1:
                        continue
                    slot = chain.at[way, s, streams[half]]
                    if s > 0:
                        flying[way, half].wait_recv()
                    if s > last[way]:
                        continue
                    here = term(half, chunk_of(way, s))
                    if s > 0:
                        here = slot[...].astype(F32) + here
                    slot[...] = here.astype(kind)
                    flying[way, half] = send(
                        slot, chain.at[way, s + 1, streams[half]], (up, down)[way]
                    )
            if s < 8:
                yield
        for half in range(len(streams)):
            total[streams[half], :] = (
                term(half, z)
                + chain[0, 8, streams[half], :].astype(F32)
                + chain[1, 7, streams[half], :].astype(F32)
            )

    def share_of(buf, d):
        return buf.at[:, pl.ds(pl.multiple_of(rem(z + d, ZN) * CH, 16), CH), :]

    def gather_ring(buf):
        for s in range(8):
            ref = share_of(buf, -s)
            copies = [send(ref, ref, up)]
            if s < 7:
                ref = share_of(buf, s)
                copies.append(send(ref, ref, down))
            yield
            wait(copies)

    target = helpers[g]
    sib_target = helpers[sib]

    def plane_sum(plane, cross, total, rows):
        lo, hi = pl.ds(0, CH), pl.ds(CH, rows - CH)
        plane[y, x] = total[...].astype(plane.dtype)

        def item(dx, dy, *part):
            return plane.at[(rem(y + dy, 4), rem(x + dx, 4), *part)]

        own = item(0, 0)
        first = {step: send(own, own, peer) for step, peer in around.items()}
        yield
        passed = []

        def relay(step, source, part):
            ref = item(*source, part)
            passed.append(send(ref, ref, around[step]))

        for step in first:
            first[step].wait_recv()
        for side in (0, 1, -1):
            relay((1, 0), (-1, side), lo)
            relay((0, 1), (side, -1), lo)
            relay((-1, 0), (1, side), hi)
            relay((0, -1), (side, 1), hi)
        relay((1, 1), (-1, -1), lo)
        relay((-1, 1), (1, -1), hi)
        yield
        wait(passed)

        def sums(me, its_target):
            def step(slot, carry):
                b, a = lax.div(slot, 4), lax.rem(slot, 4)
                group = slot * 2 + core
                w_home = jnp.where(helpers[group] == me, 1.0, 0.0)
                w_own = jnp.where(its_target == group, 1.0, 0.0)
                w_help = jnp.where(helpers[group] == its_target, 1.0, 0.0)
                item = plane.at[b, a]
                home, helped, *tally = carry
                first, second = item[0:CH, :].astype(F32), item[CH:CG, :].astype(F32)
                home = home + w_home * second
                helped = helped + w_own * first + w_help * second
                if rows == CS:
                    count = item[CG:CS, :]
                    tally = [
                        tally[0] + w_home * count,
                        tally[1] + w_own * count,
                        tally[2] + w_help * count,
                    ]
                return (home, helped, *tally)

            zero = jnp.zeros((CH, L), F32)
            none = jnp.zeros((8, L), F32)
            carry = (zero, zero) + ((none,) * 3 if rows == CS else ())
            home, helped, *tally = lax.fori_loop(0, 16, step, carry)
            if rows == CS:
                first = jnp.broadcast_to(tally[0][4:5, :], (8, L))
                second = jnp.broadcast_to(tally[1][0:1, :] + tally[2][4:5, :], (8, L))
                where = lax.broadcasted_iota(jnp.int32, (8, L), 0) < 4
                return home, helped, jnp.where(where, first, second)
            return home, helped, None

        home, helped, tally = sums(sib, sib_target)
        cross[0, 0:CH, :] = home
        cross[0, CH:CG, :] = helped
        if rows == CS:
            cross[0, CG:CS, :] = tally
        swap = send(cross.at[0], cross.at[1], other)
        home, helped, tally = sums(g, target)
        yield
        swap.wait_recv()
        total[0:CH, :] = total[0:CH, :] + home + cross[1, 0:CH, :]
        total[CH:CG, :] = helped + cross[1, CH:CG, :]
        if rows == CS:
            where = lax.broadcasted_iota(jnp.int32, (8, L), 0) < 4
            own = jnp.where(where, total[CG:CS, :], 0.0)
            total[CG:CS, :] = own + tally + cross[1, CG:CS, :]

    def step_on(task):
        return next(task, "done") != "done"

    def finish(task):
        for _ in task:
            pass

    is_home = [(flag[r] == 0) | (target == g) for r in range(RDEV)]
    alive = [live[r].astype(F32) for r in range(RDEV)]
    home_f = [jnp.where(h, 1.0, 0.0) for h in is_home]
    help_f = [1.0 - h for h in home_f]
    home_live = [h * a for h, a in zip(home_f, alive)]
    help_live = [h * a for h, a in zip(help_f, alive)]

    first_half = (lax.broadcasted_iota(jnp.int32, (1, L), 1) < L // 2).astype(F32)
    halves = (first_half, 1.0 - first_half)

    def norm(row):
        center = jnp.sum(row, axis=-1, keepdims=True) * (1.0 / D)
        centred = row - center
        spread = jnp.sum(centred * centred, axis=-1, keepdims=True) * (1.0 / D)
        rstd = lax.rsqrt(spread + 1e-05)
        return centred * rstd, rstd

    def normalise():
        get_emb.wait()

        @pl.loop(0, RDEV)
        def _(r):
            rows = pl.ds(pl.multiple_of(r * L, L), L)
            normed[rows, :] = norm(emb[r].astype(F32))[0].astype(BF16)

    def project(m, dst):
        @pl.loop(0, 3)
        def _(n):
            cols = pl.ds(pl.multiple_of(n * 256, 256), 256)
            dst[:, cols] = dot(normed[...], weights[m, :, cols]).astype(BF16)

    def project_back():
        get_cot.wait()

        @pl.loop(0, 3)
        def _(n):
            cols = pl.ds(pl.multiple_of(n * 256, 256), 256)
            dattend[:, cols] = dot_t(cot[...].reshape(RDEV * L, D), weights[3, cols, :]).astype(
                BF16
            )

    def pair_terms(left, right, home_w, help_w, part, centre):
        masks = [
            [(half * w).astype(BF16) for w in ws] for ws in (home_w, help_w) for half in halves
        ]

        @pl.loop(0, PAIRS)
        def _(p):
            cols = pl.ds(pl.multiple_of(p * L, L), L)
            lefts = jnp.concatenate(
                [left[r * L : (r + 1) * L, cols] for r in range(RDEV)], axis=1
            )
            rights = [right[r * L : (r + 1) * L, cols] for r in range(RDEV)]
            for v in range(4):
                masked = jnp.concatenate(
                    [rights[r] * masks[v][r] for r in range(RDEV)], axis=1
                )
                rows = pl.ds(pl.multiple_of(p * 2 * L + (v % 2) * L, L), L)
                sums = dot_t(lefts, masked)
                if centre:
                    sums = sums - jnp.sum(sums, axis=-1, keepdims=True) * (1.0 / L)
                part[v // 2, rows, :] = sums

    def split_heads(ref, r, cols):
        piece = ref[r * L : (r + 1) * L, cols]
        return jnp.concatenate([piece * half.astype(BF16) for half in halves], axis=0)

    def apply_pair(mix, first, first_out, second, second_out, scale, p):
        cols = pl.ds(pl.multiple_of(p * L, L), L)
        tiles = [
            [mix[e, pl.ds(pl.multiple_of((2 * p + h) * L, L), L), :] for h in range(2)]
            for e in range(2)
        ]
        straight = [jnp.concatenate(t, axis=1) for t in tiles]
        turned = [jnp.concatenate([t.T for t in ts], axis=1) for ts in tiles]
        for r in range(RDEV):
            rows = slice(r * L, (r + 1) * L)
            pick = jnp.where(is_home[r], straight[0], straight[1])
            one = dot(pick, split_heads(first, r, cols))
            pick = jnp.where(is_home[r], turned[0], turned[1])
            two = dot(pick, split_heads(second, r, cols))
            if scale is not None:
                one, two = one * scale[r], two * scale[r]
            first_out[rows, cols] = one.astype(BF16)
            second_out[rows, cols] = two.astype(BF16)

    relay = weight_relay()
    step_on(relay)
    normalise()
    finish(relay)

    project(0, queries)
    project(1, keys)
    pair_terms(queries, keys, home_live, help_live, s_part, False)

    where = lax.broadcasted_iota(jnp.int32, (8, L), 0) < 4
    home_count = home_live[0] + home_live[1] + home_live[2] + home_live[3]
    help_count = help_live[0] + help_live[1] + help_live[2] + help_live[3]
    counts = jnp.where(where, home_count, help_count)
    scalings = []
    own_share = pl.ds(pl.multiple_of(z * CH, 16), CH)

    def score_task():
        yield from chain_sum(s_part, s_chain, s_tot, counts)
        yield from plane_sum(s_plane, s_cross, s_tot, CS)
        for e in range(2):
            depth = s_tot[CG + 4 * e : CG + 4 * e + 1, :]
            scalings.append(1.0 / (8.0 * jnp.sqrt(depth)))
            logits = s_tot[e * CH : (e + 1) * CH, :] * scalings[e]
            top = jnp.exp(logits - jnp.max(logits, axis=-1, keepdims=True))
            share = top / jnp.sum(top, axis=-1, keepdims=True)
            attend[e] = share
            probs[e, own_share, :] = share.astype(BF16)
        yield from gather_ring(probs)

    def grad_task():
        yield from chain_sum(g_part, g_chain, g_tot, None)
        yield from plane_sum(g_plane, g_cross, g_tot, CG)
        for e in range(2):
            share = attend[e]
            grads = g_tot[e * CH : (e + 1) * CH, :]
            mean = jnp.sum(grads * share, axis=-1, keepdims=True)
            dlog[e, own_share, :] = (share * (grads - mean) * scalings[e]).astype(BF16)
        yield from gather_ring(dlog)

    scores, grads = score_task(), grad_task()
    step_on(scores)
    project(2, values)
    project_back()
    pair_terms(dattend, values, home_f, help_f, g_part, True)
    for _ in range(8):
        step_on(scores)
        step_on(grads)
    for task in (grads, scores, grads, scores, grads):
        step_on(task)
    for _ in range(8):
        step_on(scores)
        step_on(grads)
    finish(scores)

    @pl.loop(0, PAIRS)
    def _(p):
        apply_pair(probs, values, attended, dattend, dvalue, None, p)

    @pl.loop(0, 3)
    def _(n):
        cols = pl.ds(pl.multiple_of(n * 256, 256), 256)
        part = dot(attended[...], weights[3, :, cols])
        for r in range(RDEV):
            rows = slice(r * L, (r + 1) * L)
            out[r, :, cols] = (emb[r, :, cols].astype(F32) + part[rows, :]).astype(BF16)

    put_out = pltpu.make_async_copy(out, out_ref, own_sems.at[6])
    put_out.start()

    @pl.loop(0, 3)
    def _(n):
        cols = pl.ds(pl.multiple_of(n * 256, 256), 256)
        dnormed[:, cols] = dot_t(dvalue[...], weights[2, cols, :])

    finish(grads)

    @pl.loop(0, PAIRS)
    def _(p):
        apply_pair(dlog, keys, dquery, queries, dkey, alive, p)

    @pl.loop(0, 3)
    def _(n):
        cols = pl.ds(pl.multiple_of(n * 256, 256), 256)
        dnormed[:, cols] += dot_t(dquery[...], weights[0, cols, :]) + dot_t(
            dkey[...], weights[1, cols, :]
        )

    @pl.loop(0, RDEV)
    def _(r):
        rows = pl.ds(pl.multiple_of(r * L, L), L)
        unit, rstd = norm(emb[r].astype(F32))
        grad = dnormed[rows, :]
        mean = jnp.sum(grad, axis=-1, keepdims=True) * (1.0 / D)
        along = jnp.sum(grad * unit, axis=-1, keepdims=True) * (1.0 / D)
        back = rstd * (grad - mean - unit * along)
        gin[r] = (cot[r].astype(F32) + back).astype(BF16)
        pltpu.make_async_copy(gin.at[r], gin_ref.at[r], own_sems.at[7 + r]).start()

    put_out.wait()
    for r in range(RDEV):
        pltpu.make_async_copy(gin.at[r], gin_ref.at[r], own_sems.at[7 + r]).wait()

    for copy in started:
        copy.wait_send()


def per_device(*args):
    rows = RDEV * L
    hbm = pl.BlockSpec(memory_space=pl.ANY)
    smem = pl.BlockSpec(memory_space=pltpu.SMEM)
    shape = jax.ShapeDtypeStruct((RDEV, L, D), BF16)
    flat = pltpu.VMEM((rows, D), BF16)
    scratch = [
        pltpu.VMEM((RDEV, L, D), BF16),
        pltpu.VMEM((RDEV, L, D), BF16),
        pltpu.VMEM((RDEV, L, D), BF16),
        pltpu.VMEM((RDEV, L, D), BF16),
        pltpu.VMEM((4, D, D), BF16),
        flat,
        flat,
        flat,
        flat,
        flat,
        pltpu.VMEM((2, HEADS * L, L), F32),
        pltpu.VMEM((2, HEADS * L, L), F32),
        pltpu.VMEM((2, 9, CS, L), F32),
        pltpu.VMEM((2, 9, CG, L), BF16),
        pltpu.VMEM((4, 4, CS, L), F32),
        pltpu.VMEM((4, 4, CG, L), BF16),
        pltpu.VMEM((2, CS, L), F32),
        pltpu.VMEM((2, CG, L), F32),
        pltpu.VMEM((CS, L), F32),
        pltpu.VMEM((CG, L), F32),
        pltpu.VMEM((2, CH, L), F32),
        pltpu.VMEM((2, HEADS * L, L), BF16),
        pltpu.VMEM((2, HEADS * L, L), BF16),
        flat,
        flat,
        flat,
        flat,
        pltpu.VMEM((rows, D), F32),
        pltpu.SemaphoreType.DMA((N_SEM,)),
        pltpu.SemaphoreType.DMA((N_SEM,)),
        pltpu.SemaphoreType.DMA((11,)),
    ]
    return pl.pallas_call(
        kernel,
        out_shape=(shape, shape),
        in_specs=[hbm] * 6 + [smem] * 3,
        out_specs=(hbm, hbm),
        scratch_shapes=scratch,
        compiler_params=pltpu.CompilerParams(
            collective_id=0, has_side_effects=True, vmem_limit_bytes=56 * 1024 * 1024
        ),
    )(*args)


def solution(mesh):
    placed = (
        P(("grp", "row"), None, None),
        P(("grp", "row"), None, None),
        P("row", None),
        P("row", None),
        P("row", None),
        P("row", None),
        P(),
        P(("grp", "row")),
        P(("grp", "row")),
    )
    return jax.shard_map(
        per_device,
        mesh=mesh,
        in_specs=placed,
        out_specs=(P(("grp", "row"), None, None), P(("grp", "row"), None, None)),
        check_vma=False,
    )
```

time: 756 us -> 146 us (0.19)
  waiting for transfers between devices: 439 us -> 0 us
  blocking collectives: 246 us -> 0 us
  Pallas kernels: 0 us -> 142 us
  matrix products: 19.3 us -> 0 us
  between operations: 18 us -> 0.65 us
  local copies, waits for them, and re-layouts: 18.8 us -> 3.02 us
  other arithmetic: 13.2 us -> 0 us
    all_gather x6 -> x0, waiting for transfers between devices: 300 us -> none  [the longest x1 70.3 us: per_device(): lax.all_gather(w_value, 'row', axis=0, tiled=True)]
    all_gather x7 -> x0, blocking collectives: 218 us -> none  [the longest x1 49.4 us: per_device(): lax.all_gather(counted[1], 'grp', axis=0, tiled=True)]
    pallas_call x0 -> x1, Pallas kernels: none -> 142 us  [per_device(): pl.pallas_call(kernel, out_shape=(shape, shape), in_specs=[hbm] * 6 + [sm...]
    reduce_scatter x2 -> x0, waiting for transfers between devices: 136 us -> none  [the longest x1 70.9 us: per_device(): lax.psum_scatter(scores_part, 'row', scatter_dimension=2, tiled=True)]
    unnamed x1 -> x0, blocking collectives: 28.6 us -> none
    dot_general x16 -> x0, matrix products: 19.3 us -> none  [the longest x4 4.93 us: times_transpose(): lax.dot_general(left, weight, (((1,), (1,)), ((), ())), preferred_element...]
  transfers between devices with their start and end apart: 8 -> 0, of which waited for: 7 -> 0; matrix products, arithmetic and copies ran while one was open for 4% -> 0% of each run, Pallas kernels for 0% -> 0%
where the time goes in v1:
time: 146 us
  Pallas kernels  142 us (97%)
  local copies, waits for them, and re-layouts  3.02 us (2%)
    pallas_call x1, Pallas kernels, per_device(): pl.pallas_call(kernel, out_shape=(shape, shape), in_specs=[hbm] * 6 + [sm...  142 us
    unnamed x4, local copies, waits for them, and re-layouts  3.02 us

profile of v1, /device:TPU:6, one launch (start us, length us, event | category | flops | bytes accessed | tf_op | source)
XLA Modules:
  0.0 145.7 jit_solution(12116759249659745045)
XLA Ops:
  0.6 142.0 %shard_map.104 = (bf16[4,128,768]{2,1,0:T(8,128)(2,1)}, bf16[4,128,768]{2,1,0:T(8,128)(2,1)}) custom-call(bf16[4,128,768]{2,1,0:T(8,128)(2,1)} %emb_in.1, bf16[4,128,768]{2,1,0:T(8,128)(2,1)} %cot_in.1, bf16[48,768]{1,0:T(8,128)(2,1)} %w_query.1, bf16[48,768]{1,0:T(8,128)(2,1)} %w_key.1, bf16[48,768]{1,0:T(8,128)(2,1)} %w_value.1, bf16[48,768]{1,0:T(8,128)(2,1)} %w_output.1, ...), custom_call_target="tpu_custom_call" | custom-call | tf_op jit(solution)/shard_map/pallas_call | solution.py:588
  142.7 0.0 copy-start
  142.7 2.1 %copy.13 = bf16[4,128,768]{2,1,0:T(8,128)(2,1)} copy(bf16[4,128,768]{2,1,0:T(8,128)(2,1)} %get-tuple-element.4) | data formatting | bytes 1572864
  144.8 0.0 copy-done
  144.8 0.9 copy.14
Async XLA Ops:
  142.7 2.1 %copy-start = (bf16[4,128,768]{2,1,0:T(8,128)(2,1)S(1)}, bf16[4,128,768]{2,1,0:T(8,128)(2,1)}, u32[]{:S(2)}) copy-start(bf16[4,128,768]{2,1,0:T(8,128)(2,1)} %get-tuple-element.5) | copy-start | bytes 2359300

commit v2 on v1

v2 whole, which is shorter than its diff:
```python
import functools

import jax
import jax.numpy as jnp
from jax import lax
from jax.experimental import pallas as pl
from jax.experimental.pallas import tpu as pltpu
from jax.sharding import PartitionSpec as P

HEADS = 12
RDEV = 4
L = 128
D = 768
ZN = 16
SH = D // ZN
QC = D // 2
CH = HEADS * L // ZN
PAIRS = HEADS // 2
MESH = pl.DeviceIdType.MESH
F32 = jnp.float32
BF16 = jnp.bfloat16
N_SEM = 400

PARTS = 2
PR = CH // PARTS
HALF = HEADS * L // PARTS
PP = PAIRS // PARTS
CHUNK = 3
S_STREAMS = 2
G_STREAMS = 1

W_TREE = {0: (3, 1, 2), 3: (3, 1, 2), 6: (1, 2)}
Z_TREE = {
    0: (3, -3, 1, -1),
    -3: (3, 1, -1),
    3: (-3, -1, 1),
    -6: (1, -1),
    6: (-1, 1),
    -7: (1,),
}
S_TREE = {0: (1, 2), **{k: (1,) for k in range(2, 8)}}
G_TREE = {k: (1,) for k in range(8)}
S_LEAD = 12
HOLD = 2
Z_HOPS = (1, -1, 2, -2, 3, -3)


class Plan:
    def __init__(self):
        self.now = 0.0
        self.free = {}
        self.tasks = []
        self.out = []
        self.marks = {}

    def book(self, kb, path):
        self.now += 0.1
        start, hops = self.now, 0
        for link, units, cores in path:
            hops += units
            span = kb / 600.0 if link == "core" else units * kb * cores / 100.0
            start = max(start, self.free.get(link, 0.0)) + span
            self.free[link] = start
        return start + 2.5 + 0.15 * (hops - 1)

    def spend(self, time):
        self.now += time

    def mark(self, name):
        self.marks[name] = round(self.now, 1)

    def spawn(self, rank, task):
        wanted = next(task, None)
        if wanted is not None:
            self.tasks.append([rank, task, wanted])

    def run(self, done):
        while not done():
            best = None
            for entry in self.tasks:
                due = max([copy.due for copy in entry[2]], default=0.0)
                key = (max(due, self.now), entry[0], due)
                if best is None or key < best[0]:
                    best = (key, entry)
            key, entry = best
            while self.out and self.now + 0.1 < key[0] and self.out[0].due < self.now:
                self.out.pop(0).copy.wait_send()
                self.now += 0.03
            self.now = max(self.now, key[0]) + 0.05 * len(entry[2])
            for copy in entry[2]:
                copy.wait()
            wanted = next(entry[1], None)
            if wanted is None:
                self.tasks.remove(entry)
            else:
                entry[2] = wanted


LAST_PLAN = []


class Flight:
    def __init__(self, copy, due):
        self.copy, self.due = copy, due

    def wait(self):
        self.copy.wait_recv()


def rem(a, n):
    return lax.rem(a + n, n)


def dot(a, b):
    return lax.dot_general(a, b, (((1,), (0,)), ((), ())), preferred_element_type=F32)


def dot_t(a, b):
    return lax.dot_general(a, b, (((1,), (1,)), ((), ())), preferred_element_type=F32)


def kernel(
    emb_in,
    cot_in,
    w_query,
    w_key,
    w_value,
    w_output,
    helpers,
    flag,
    live,
    out_ref,
    gin_ref,
    emb,
    cot,
    out,
    gin,
    weights,
    normed,
    queries,
    keys,
    values,
    dattend,
    s_part,
    g_part,
    s_chain,
    g_chain,
    s_plane,
    g_plane,
    s_cross,
    g_cross,
    s_tot,
    g_tot,
    attend,
    probs,
    dlog,
    attended,
    dquery,
    dkey,
    dvalue,
    dnormed,
    send_sems,
    recv_sems,
    own_sems,
):
    g = lax.axis_index("grp")
    z = lax.axis_index("row")
    core = lax.rem(g, 2)
    x = lax.rem(lax.div(g, 2), 4)
    y = lax.div(g, 8)
    sib = g + 1 - 2 * core
    way_of_core = 1 - 2 * core
    plan = Plan()
    LAST_PLAN[:] = [plan]

    def at(group, row):
        return {"grp": group, "row": row}

    def chip(dx, dy):
        return at((rem(y + dy, 4) * 4 + rem(x + dx, 4)) * 2 + core, z)

    hops = {d: at(g, rem(z + d, ZN)) for d in Z_HOPS}
    around = {
        (dx, dy): chip(dx, dy) for dx in (1, -1, 0) for dy in (1, -1, 0) if dx != 0 or dy != 0
    }
    other = at(sib, z)
    x_step = 1 - 2 * lax.rem(x + core, 2)
    y_step = 1 - 2 * lax.rem(y + core, 2)
    partners = (
        (chip(x_step, 0), (("wx", 1, 1),)),
        (chip(0, y_step), (("wy", 1, 1),)),
        (chip(x_step, y_step), (("wx", 1, 1), ("wy", 1, 1))),
    )

    barrier = pltpu.get_barrier_semaphore()
    peers = [*hops.values(), *around.values(), other]
    for peer in peers:
        pl.semaphore_signal(barrier, inc=1, device_id=peer, device_id_type=MESH)

    started = [0]
    steps = [0]

    def send(ref, dst, peer, kb, path):
        index = started[0]
        copy = pltpu.make_async_remote_copy(
            src_ref=ref,
            dst_ref=dst,
            send_sem=send_sems.at[index],
            recv_sem=recv_sems.at[index],
            device_id=peer,
            device_id_type=MESH,
        )
        copy.start()
        started[0] += 1
        flight = Flight(copy, plan.book(kb, path))
        plan.out.append(flight)
        return flight

    own_rows = pl.ds(pl.multiple_of(z * SH, 16), SH)
    shards = [
        pltpu.make_async_copy(ref, weights.at[m, own_rows, :], own_sems.at[m])
        for m, ref in enumerate((w_query, w_key, w_value, w_output))
    ]
    get_emb = pltpu.make_async_copy(emb_in, emb, own_sems.at[4])
    get_cot = pltpu.make_async_copy(cot_in, cot, own_sems.at[5])
    for copy in (*shards, get_emb, get_cot):
        copy.start()
    for copy in shards:
        copy.wait()

    pl.semaphore_wait(barrier, len(peers))

    arrived = [0, 0]

    def weight_set(m, rank):
        def rows(k):
            return pl.ds(pl.multiple_of(rem(z - way_of_core * k, ZN) * SH, 16), SH)

        def piece(k):
            columns = pl.ds(pl.multiple_of(lax.rem(x, 2) * QC, 128), QC)
            return weights.at[2 * m + lax.rem(y, 2), rows(k), columns]

        def forward(k):
            for hop in W_TREE.get(k, ()):
                ref = piece(k)
                peer = at(g, rem(z + way_of_core * hop, ZN))
                path = (("up", hop, 1),)
                flight = send(ref, ref, peer, 36.9, path)
                plan.free["down"] = plan.free.get("down", 0.0) + hop * 0.369
                plan.spawn(rank, arrive(k + hop, flight))

        def arrive(k, flight):
            yield [flight]
            forward(k)
            ref = piece(k)
            flights = [send(ref, ref, peer, 36.9, path) for peer, path in partners]
            yield flights
            if k < 8:
                ref = weights.at[pl.ds(2 * m, 2), rows(k), :]
                yield [send(ref, ref, other, 147.5, (("core", 1, 1),))]
            arrived[m] += 1

        forward(0)

    def chain_sum(part, chain, tree, p, counts, streams, rank, finished):
        kind = chain.dtype
        rows = chain.shape[3]
        edges = [0, rows] if streams == 1 else [0, PR, rows]
        left = [2 * streams]

        def term(lo, hi, chunk):
            span = pl.ds(pl.multiple_of(p * HALF + chunk * PR, 16), PR)
            pieces = []
            if lo < PR:
                pieces.append(part[0, span, :])
            if hi > PR:
                pieces.append(part[1, span, :])
            if hi > 2 * PR:
                pieces.append(counts)
            return jnp.concatenate(pieces, axis=0) if len(pieces) > 1 else pieces[0]

        nodes = (8, 7)
        below = [
            {
                k: [k + hop for hop in tree.get(k, ()) if k + hop <= nodes[way]]
                for k in range(nodes[way] + 1)
            }
            for way in range(2)
        ]

        def stream(way, lo, hi):
            span = pl.ds(lo, hi - lo)
            kb = (hi - lo) * L * (4 if kind == F32 else 2) / 1000.0
            sign = 1 - 2 * way
            above = {child: k for k, under in below[way].items() for child in under}
            flights = {}

            def pass_on(k):
                here = term(lo, hi, rem(z + sign * k, ZN))
                for child in below[way][k]:
                    here = here + chain[p, way, child - 1, span].astype(F32)
                slot = chain.at[p, way, 7 + k, span]
                slot[...] = here.astype(kind)
                plan.spend(0.04)
                hop = k - above[k]
                path = (("up" if way == 0 else "down", hop, 2),)
                landing = chain.at[p, way, k - 1, span]
                flights[k] = send(slot, landing, hops[sign * hop], kb, path)
                if all(child in flights for child in below[way][above[k]]):
                    plan.spawn(rank, node(above[k]))

            def node(k):
                yield [flights[child] for child in below[way][k]]
                if k > 0:
                    if kind == F32:
                        steps[0] += 1
                        lead()
                    pass_on(k)
                    return
                left[0] -= 1
                if left[0] == 0:
                    plan.spend(0.1)
                    total = term(0, rows, z)
                    for side in range(2):
                        for child in below[side][0]:
                            total = total + chain[p, side, child - 1].astype(F32)
                    finished(p, total)

            for k in range(nodes[way], 0, -1):
                if not below[way][k]:
                    pass_on(k)

        for lo, hi in zip(edges[:-1], edges[1:]):
            for way in range(2):
                stream(way, lo, hi)

    def spread(buf, tree, p, rank, finished):
        left = [15]

        def piece(d):
            start = pl.multiple_of(p * HALF + rem(z + d, ZN) * PR, 16)
            return buf.at[:, pl.ds(start, PR), :]

        def forward(d):
            for hop in tree.get(d, ()):
                ref = piece(d)
                path = (("up", hop, 2),) if hop > 0 else (("down", -hop, 2),)
                flight = send(ref, ref, hops[hop], PR * 0.512, path)
                plan.spawn(rank, arrive(d - hop, flight))

        def arrive(d, flight):
            yield [flight]
            forward(d)
            left[0] -= 1
            if left[0] == 0:
                finished(p)

        forward(0)

    target = helpers[g]
    sib_target = helpers[sib]
    top_half = lax.broadcasted_iota(jnp.int32, (8, L), 0) < 4

    def plane_sum(plane, cross, total, p, rank, finished):
        rows = 2 * PR + (8 if p == 0 and plane.dtype == F32 else 0)
        tallied = rows > 2 * PR
        kb = rows * L * (4 if plane.dtype == F32 else 2) / 1000.0
        lo, hi = pl.ds(0, PR), pl.ds(PR, rows - PR)
        passed = []
        left = [8]
        whole = pl.ds(0, rows)
        plane[p, y, x, whole] = total[p, whole].astype(plane.dtype)

        def path(dx, dy):
            steps = []
            if dx != 0:
                steps.append(("x+" if dx > 0 else "x-", 1, 2))
            if dy != 0:
                steps.append(("y+" if dy > 0 else "y-", 1, 2))
            return steps

        def item(dx, dy, *span):
            return plane.at[(p, rem(y + dy, 4), rem(x + dx, 4), *span)]

        def relay(step, source, span, share):
            ref = item(*source, span)
            passed.append(send(ref, ref, around[step], kb * share, path(*step)))

        def arrive(dx, dy, flight):
            yield [flight]
            source = (-dx, -dy)
            if dx != 0:
                relay((dx, 0), source, lo if dx > 0 else hi, 0.5)
            if dy != 0:
                relay((0, dy), source, lo if dy > 0 else hi, 0.5)
            if (dx, dy) == (1, 1):
                relay((1, 1), source, lo, 0.5)
            if (dx, dy) == (-1, 1):
                relay((-1, 1), source, hi, 0.5)
            left[0] -= 1
            if left[0] == 0:
                plan.spawn(rank, finish())
                if plane.dtype == F32:
                    state["sent"] += 1
                    release()

        def sums(me, its_target):
            def step(slot, carry):
                b, a = lax.div(slot, 4), lax.rem(slot, 4)
                group = slot * 2 + core
                w_home = jnp.where(helpers[group] == me, 1.0, 0.0)
                w_own = jnp.where(its_target == group, 1.0, 0.0)
                w_help = jnp.where(helpers[group] == its_target, 1.0, 0.0)
                share = plane.at[p, b, a]
                home, helped, *tally = carry
                first, second = share[0:PR, :].astype(F32), share[PR : 2 * PR, :].astype(F32)
                home = home + w_home * second
                helped = helped + w_own * first + w_help * second
                if tallied:
                    count = share[2 * PR : rows, :]
                    tally = [
                        tally[0] + w_home * count,
                        tally[1] + w_own * count,
                        tally[2] + w_help * count,
                    ]
                return (home, helped, *tally)

            zero = jnp.zeros((PR, L), F32)
            none = jnp.zeros((8, L), F32)
            carry = (zero, zero) + ((none,) * 3 if tallied else ())
            home, helped, *tally = lax.fori_loop(0, 16, step, carry)
            plan.spend(0.6 / PARTS)
            if tallied:
                first = jnp.broadcast_to(tally[0][4:5, :], (8, L))
                second = jnp.broadcast_to(tally[1][0:1, :] + tally[2][4:5, :], (8, L))
                return home, helped, jnp.where(top_half, first, second)
            return home, helped, None

        def finish():
            yield list(passed)
            home, helped, tally = sums(sib, sib_target)
            cross[p, 0, 0:PR, :] = home
            cross[p, 0, PR : 2 * PR, :] = helped
            if tallied:
                cross[p, 0, 2 * PR : rows, :] = tally
            swap = send(cross.at[p, 0, whole], cross.at[p, 1, whole], other, rows * 0.512, (("core", 1, 1),))
            home, helped, tally = sums(g, target)
            yield [swap]
            total[p, 0:PR, :] = total[p, 0:PR, :] + home + cross[p, 1, 0:PR, :]
            total[p, PR : 2 * PR, :] = helped + cross[p, 1, PR : 2 * PR, :]
            if tallied:
                own = jnp.where(top_half, total[p, 2 * PR : rows, :], 0.0)
                total[p, 2 * PR : rows, :] = own + tally + cross[p, 1, 2 * PR : rows, :]
            plan.spend(0.1)
            finished(p)

        for step, peer in around.items():
            own = item(0, 0, whole)
            plan.spawn(rank, arrive(*step, send(own, own, peer, kb, path(*step))))

    is_home = [(flag[r] == 0) | (target == g) for r in range(RDEV)]
    alive = [live[r].astype(F32) for r in range(RDEV)]
    home_f = [jnp.where(h, 1.0, 0.0) for h in is_home]
    help_f = [1.0 - h for h in home_f]
    home_live = [h * a for h, a in zip(home_f, alive)]
    help_live = [h * a for h, a in zip(help_f, alive)]
    home_count = home_live[0] + home_live[1] + home_live[2] + home_live[3]
    help_count = help_live[0] + help_live[1] + help_live[2] + help_live[3]
    counts = jnp.where(top_half, home_count, help_count)

    first_half = (lax.broadcasted_iota(jnp.int32, (1, L), 1) < L // 2).astype(F32)
    halves = (first_half, 1.0 - first_half)

    def norm(row):
        center = jnp.sum(row, axis=-1, keepdims=True) * (1.0 / D)
        centred = row - center
        spread_of = jnp.sum(centred * centred, axis=-1, keepdims=True) * (1.0 / D)
        rstd = lax.rsqrt(spread_of + 1e-05)
        return centred * rstd, rstd

    def normalise():
        plan.spend(1.2)

        @pl.loop(0, RDEV)
        def _(r):
            rows = pl.ds(pl.multiple_of(r * L, L), L)
            normed[rows, :] = norm(emb[r].astype(F32))[0].astype(BF16)

    def project(m, dst, p):
        plan.spend(0.5)

        @pl.loop(0, 2)
        def _(n):
            rows = pl.ds(pl.multiple_of(n * 256, 256), 256)
            cols = pl.ds(p * QC, QC)
            dst[rows, cols] = dot(normed[rows, :], weights[m, :, cols]).astype(BF16)

    def project_back():
        plan.spend(0.8)

        @pl.loop(0, 3)
        def _(n):
            cols = pl.ds(pl.multiple_of(n * 256, 256), 256)
            dattend[:, cols] = dot_t(cot[...].reshape(RDEV * L, D), weights[3, cols, :]).astype(
                BF16
            )

    def pair_terms(left, right, home_w, help_w, part, centre, first, last):
        plan.spend(0.1 * (last - first))
        masks = [
            [(half * w).astype(BF16) for w in ws] for ws in (home_w, help_w) for half in halves
        ]

        @pl.loop(first, last)
        def _(p):
            cols = pl.ds(pl.multiple_of(p * L, L), L)
            lefts = jnp.concatenate(
                [left[r * L : (r + 1) * L, cols] for r in range(RDEV)], axis=1
            )
            rights = [right[r * L : (r + 1) * L, cols] for r in range(RDEV)]
            for v in range(4):
                masked = jnp.concatenate(
                    [rights[r] * masks[v][r] for r in range(RDEV)], axis=1
                )
                rows = pl.ds(pl.multiple_of(p * 2 * L + (v % 2) * L, L), L)
                sums = dot_t(lefts, masked)
                if centre:
                    sums = sums - jnp.sum(sums, axis=-1, keepdims=True) * (1.0 / L)
                part[v // 2, rows, :] = sums

    def split_heads(ref, r, cols):
        piece = ref[r * L : (r + 1) * L, cols]
        return jnp.concatenate([piece * half.astype(BF16) for half in halves], axis=0)

    def apply_pair(mix, first, first_out, second, second_out, scale, p):
        cols = pl.ds(pl.multiple_of(p * L, L), L)
        tiles = [
            [mix[e, pl.ds(pl.multiple_of((2 * p + h) * L, L), L), :] for h in range(2)]
            for e in range(2)
        ]
        straight = [jnp.concatenate(t, axis=1) for t in tiles]
        turned = [jnp.concatenate([t.T for t in ts], axis=1) for ts in tiles]
        for r in range(RDEV):
            rows = slice(r * L, (r + 1) * L)
            pick = jnp.where(is_home[r], straight[0], straight[1])
            one = dot(pick, split_heads(first, r, cols))
            pick = jnp.where(is_home[r], turned[0], turned[1])
            two = dot(pick, split_heads(second, r, cols))
            if scale is not None:
                one, two = one * scale[r], two * scale[r]
            first_out[rows, cols] = one.astype(BF16)
            second_out[rows, cols] = two.astype(BF16)

    held = []
    state = {"sent": 0, "soft": set(), "grad": set(), "probs": 0, "dlog": 0, "applied": False}
    state.update(terms=False, led=False, late=list(range(PARTS)))
    scalings = []
    put_out = pltpu.make_async_copy(out, out_ref, own_sems.at[6])

    def share_rows(p):
        return pl.ds(pl.multiple_of(p * HALF + z * PR, 16), PR)

    def scores_summed(p, total):
        s_tot[p, 0 : total.shape[0], :] = total
        plan.mark(("scores summed", p))
        plane_sum(s_plane, s_cross, s_tot, p, 1, soften)

    def grads_summed(p, total):
        g_tot[p] = total
        plan.mark(("grads summed", p))
        held.append(p)
        release()

    def release():
        while held and state["sent"] >= HOLD:
            plane_sum(g_plane, g_cross, g_tot, held.pop(0), 2, grads_known)

    def soften(p):
        plan.spend(0.5 / PARTS)
        plan.mark(("softmax", p))
        for e in range(2):
            if p == 0:
                depth = s_tot[0, 2 * PR + 4 * e : 2 * PR + 4 * e + 1, :]
                scalings.append(1.0 / (8.0 * jnp.sqrt(depth)))
            logits = s_tot[p, e * PR : (e + 1) * PR, :] * scalings[e]
            top = jnp.exp(logits - jnp.max(logits, axis=-1, keepdims=True))
            share = top / jnp.sum(top, axis=-1, keepdims=True)
            attend[e, p * PR : (p + 1) * PR, :] = share
            probs[e, share_rows(p), :] = share.astype(BF16)
        state["soft"].add(p)
        spread(probs, Z_TREE, p, 3, probs_here)
        differentiate(p)

    def grads_known(p):
        state["grad"].add(p)
        differentiate(p)

    def differentiate(p):
        if p not in state["soft"] or p not in state["grad"]:
            return
        plan.spend(0.4 / PARTS)
        plan.mark(("dlogit", p))
        for e in range(2):
            share = attend[e, p * PR : (p + 1) * PR, :]
            grads = g_tot[p, e * PR : (e + 1) * PR, :]
            mean = jnp.sum(grads * share, axis=-1, keepdims=True)
            dlog[e, share_rows(p), :] = (share * (grads - mean) * scalings[e]).astype(BF16)
        spread(dlog, Z_TREE, p, 2, dlog_here)

    def probs_here(p):
        plan.mark(("probs", p))
        plan.spawn(9, apply_probs(p))

    def dlog_here(p):
        state["dlog"] += 1
        plan.mark(("dlog", p))
        if state["dlog"] < PARTS:
            state["late"].remove(p)
            plan.spawn(8, apply_dlog(p))

    def in_chunks(p, work):
        for first in range(p * PP, p * PP + PP, CHUNK):
            plan.spend(0.5 * CHUNK)

            @pl.loop(first, first + CHUNK)
            def _(pair):
                work(pair)

            yield []

    def apply_dlog(p):
        yield []
        yield from in_chunks(
            p, lambda pair: apply_pair(dlog, keys, dquery, queries, dkey, alive, pair)
        )

    def apply_probs(p):
        yield []
        yield from in_chunks(
            p, lambda pair: apply_pair(probs, values, attended, dattend, dvalue, None, pair)
        )
        state["probs"] += 1
        if state["probs"] < PARTS:
            return
        plan.spend(0.8)

        @pl.loop(0, 3)
        def _(n):
            cols = pl.ds(pl.multiple_of(n * 256, 256), 256)
            part = dot(attended[...], weights[3, :, cols])
            for r in range(RDEV):
                rows = slice(r * L, (r + 1) * L)
                out[r, :, cols] = (emb[r, :, cols].astype(F32) + part[rows, :]).astype(BF16)

        put_out.start()
        yield []
        plan.spend(0.8)

        @pl.loop(0, 3)
        def _(n):
            cols = pl.ds(pl.multiple_of(n * 256, 256), 256)
            dnormed[:, cols] = dot_t(dvalue[...], weights[2, cols, :])

        state["applied"] = True

    def grad_terms():
        yield []
        get_cot.wait()
        for p in range(PARTS):
            project(2, values, p)
            yield []
        project_back()
        yield []
        for p in range(PARTS):
            pair_terms(
                dattend, values, home_f, help_f, g_part, True, p * PP, p * PP + PP
            )
            yield []
        state["terms"] = True
        lead()

    def lead():
        if state["terms"] and steps[0] >= S_LEAD and not state["led"]:
            state["led"] = True
            for p in range(PARTS):
                chain_sum(g_part, g_chain, G_TREE, p, None, G_STREAMS, 2, grads_summed)

    plan.spend(3.0)
    weight_set(0, 0)
    weight_set(1, 4)
    get_emb.wait()
    normalise()
    plan.run(lambda: arrived[0] == 8)
    plan.mark("weights 0")
    for p in range(PARTS):
        project(0, queries, p)
        project(1, keys, p)
        pair_terms(queries, keys, home_live, help_live, s_part, False, p * PP, p * PP + PP)
        chain = s_chain.at[:, :, :, 0 : 2 * PR + (8 if p == 0 else 0)]
        chain_sum(s_part, chain, S_TREE, p, counts, S_STREAMS, 1, scores_summed)
    plan.run(lambda: arrived[1] == 8)
    plan.mark("weights 1")
    plan.spawn(9, grad_terms())
    plan.run(lambda: state["dlog"] == PARTS and not plan.tasks)
    plan.mark("all here")
    plan.spend(1.5 * len(state["late"]) + 1.6 + 1.5 + 1.0)

    for p in state["late"]:

        @pl.loop(p * PP, p * PP + PP)
        def _(pair):
            apply_pair(dlog, keys, dquery, queries, dkey, alive, pair)

    @pl.loop(0, 3)
    def _(n):
        cols = pl.ds(pl.multiple_of(n * 256, 256), 256)
        dnormed[:, cols] += dot_t(dquery[...], weights[0, cols, :]) + dot_t(
            dkey[...], weights[1, cols, :]
        )

    @pl.loop(0, RDEV)
    def _(r):
        rows = pl.ds(pl.multiple_of(r * L, L), L)
        unit, rstd = norm(emb[r].astype(F32))
        grad = dnormed[rows, :]
        mean = jnp.sum(grad, axis=-1, keepdims=True) * (1.0 / D)
        along = jnp.sum(grad * unit, axis=-1, keepdims=True) * (1.0 / D)
        back = rstd * (grad - mean - unit * along)
        gin[r] = (cot[r].astype(F32) + back).astype(BF16)
        pltpu.make_async_copy(gin.at[r], gin_ref.at[r], own_sems.at[7 + r]).start()

    for flight in plan.out:
        flight.copy.wait_send()
    put_out.wait()
    for r in range(RDEV):
        pltpu.make_async_copy(gin.at[r], gin_ref.at[r], own_sems.at[7 + r]).wait()


def per_device(*args):
    rows = RDEV * L
    hbm = pl.BlockSpec(memory_space=pl.ANY)
    smem = pl.BlockSpec(memory_space=pltpu.SMEM)
    shape = jax.ShapeDtypeStruct((RDEV, L, D), BF16)
    flat = pltpu.VMEM((rows, D), BF16)
    block = pltpu.VMEM((RDEV, L, D), BF16)
    s_rows, g_rows = 2 * PR + 8, 2 * PR
    scratch = [
        block,
        block,
        block,
        block,
        pltpu.VMEM((4, D, D), BF16),
        flat,
        flat,
        flat,
        flat,
        flat,
        pltpu.VMEM((2, HEADS * L, L), F32),
        pltpu.VMEM((2, HEADS * L, L), F32),
        pltpu.VMEM((PARTS, 2, 16, s_rows, L), F32),
        pltpu.VMEM((PARTS, 2, 16, g_rows, L), BF16),
        pltpu.VMEM((PARTS, 4, 4, s_rows, L), F32),
        pltpu.VMEM((PARTS, 4, 4, g_rows, L), BF16),
        pltpu.VMEM((PARTS, 2, s_rows, L), F32),
        pltpu.VMEM((PARTS, 2, g_rows, L), F32),
        pltpu.VMEM((PARTS, s_rows, L), F32),
        pltpu.VMEM((PARTS, g_rows, L), F32),
        pltpu.VMEM((2, CH, L), F32),
        pltpu.VMEM((2, HEADS * L, L), BF16),
        pltpu.VMEM((2, HEADS * L, L), BF16),
        flat,
        flat,
        flat,
        flat,
        pltpu.VMEM((rows, D), F32),
        pltpu.SemaphoreType.DMA((N_SEM,)),
        pltpu.SemaphoreType.DMA((N_SEM,)),
        pltpu.SemaphoreType.DMA((11,)),
    ]
    return pl.pallas_call(
        kernel,
        out_shape=(shape, shape),
        in_specs=[hbm] * 6 + [smem] * 3,
        out_specs=(hbm, hbm),
        scratch_shapes=scratch,
        compiler_params=pltpu.CompilerParams(
            collective_id=0, has_side_effects=True, vmem_limit_bytes=56 * 1024 * 1024
        ),
    )(*args)


def solution(mesh):
    placed = (
        P(("grp", "row"), None, None),
        P(("grp", "row"), None, None),
        P("row", None),
        P("row", None),
        P("row", None),
        P("row", None),
        P(),
        P(("grp", "row")),
        P(("grp", "row")),
    )
    return jax.shard_map(
        per_device,
        mesh=mesh,
        in_specs=placed,
        out_specs=(P(("grp", "row"), None, None), P(("grp", "row"), None, None)),
        check_vma=False,
    )
```

time: 146 us -> 127 us (0.87)
  Pallas kernels: 142 us -> 122 us
    pallas_call x1, Pallas kernels: 142 us -> 122 us  [per_device(): pl.pallas_call(kernel, out_shape=(shape, shape), in_specs=[hbm] * 6 + [sm...]
where the time goes in v2:
time: 127 us; the launch traced here: 126 us
  Pallas kernels  122 us (96%)
  local copies, waits for them, and re-layouts  3.02 us (2%)
    pallas_call x1, Pallas kernels, per_device(): pl.pallas_call(kernel, out_shape=(shape, shape), in_specs=[hbm] * 6 + [sm...  122 us
    unnamed x4, local copies, waits for them, and re-layouts  3.02 us

profile of v2, /device:TPU:6, one launch (start us, length us, event | category | flops | bytes accessed | tf_op | source)
XLA Modules:
  0.0 126.0 jit_solution(13219639472815928126)
XLA Ops:
  0.6 122.3 %shard_map.104 = (bf16[4,128,768]{2,1,0:T(8,128)(2,1)}, bf16[4,128,768]{2,1,0:T(8,128)(2,1)}) custom-call(bf16[4,128,768]{2,1,0:T(8,128)(2,1)} %emb_in.1, bf16[4,128,768]{2,1,0:T(8,128)(2,1)} %cot_in.1, bf16[48,768]{1,0:T(8,128)(2,1)} %w_query.1, bf16[48,768]{1,0:T(8,128)(2,1)} %w_key.1, bf16[48,768]{1,0:T(8,128)(2,1)} %w_value.1, bf16[48,768]{1,0:T(8,128)(2,1)} %w_output.1, ...), custom_call_target="tpu_custom_call" | custom-call | tf_op jit(solution)/shard_map/pallas_call | solution.py:780
  123.0 0.0 copy-start
  123.0 2.1 %copy.13 = bf16[4,128,768]{2,1,0:T(8,128)(2,1)} copy(bf16[4,128,768]{2,1,0:T(8,128)(2,1)} %get-tuple-element.4) | data formatting | bytes 1572864
  125.1 0.0 copy-done
  125.1 0.9 copy.14
Async XLA Ops:
  123.0 2.1 %copy-start = (bf16[4,128,768]{2,1,0:T(8,128)(2,1)S(1)}, bf16[4,128,768]{2,1,0:T(8,128)(2,1)}, u32[]{:S(2)}) copy-start(bf16[4,128,768]{2,1,0:T(8,128)(2,1)} %get-tuple-element.5) | copy-start | bytes 2359300

commit v3 on v2

--- a/solution.py
+++ b/solution.py
@@ -45,6 +45,10 @@
 Z_HOPS = (1, -1, 2, -2, 3, -3)
 
 
+START = 0.13
+G_BLOCKS = ((0,), (1,))
+
+
 class Plan:
     def __init__(self):
         self.now = 0.0
@@ -54,7 +58,7 @@
         self.marks = {}
 
     def book(self, kb, path):
-        self.now += 0.1
+        self.now += START
         start, hops = self.now, 0
         for link, units, cores in path:
             hops += units
@@ -119,6 +123,24 @@
     return lax.dot_general(a, b, (((1,), (1,)), ((), ())), preferred_element_type=F32)
 
 
+def norm(row):
+    center = jnp.sum(row, axis=-1, keepdims=True) * (1.0 / D)
+    centred = row - center
+    spread_of = jnp.sum(centred * centred, axis=-1, keepdims=True) * (1.0 / D)
+    rstd = lax.rsqrt(spread_of + 1e-05)
+    return centred * rstd, rstd
+
+
+def finish_rows(emb, cot, proj, grads, out, gin):
+    row = emb[0].astype(F32)
+    out[0] = (row + proj[...]).astype(BF16)
+    unit, rstd = norm(row)
+    grad = grads[...]
+    mean = jnp.sum(grad, axis=-1, keepdims=True) * (1.0 / D)
+    along = jnp.sum(grad * unit, axis=-1, keepdims=True) * (1.0 / D)
+    gin[0] = (cot[0].astype(F32) + rstd * (grad - mean - unit * along)).astype(BF16)
+
+
 def kernel(
     emb_in,
     cot_in,
@@ -129,12 +151,11 @@
     helpers,
     flag,
     live,
-    out_ref,
-    gin_ref,
+    proj_ref,
+    grad_ref,
     emb,
     cot,
-    out,
-    gin,
+    proj,
     weights,
     normed,
     queries,
@@ -253,8 +274,7 @@
             yield [flight]
             forward(k)
             ref = piece(k)
-            flights = [send(ref, ref, peer, 36.9, path) for peer, path in partners]
-            yield flights
+            yield [send(ref, ref, peer, 36.9, path) for peer, path in partners]
             if k < 8:
                 ref = weights.at[pl.ds(2 * m, 2), rows(k), :]
                 yield [send(ref, ref, other, 147.5, (("core", 1, 1),))]
@@ -262,20 +282,20 @@
 
         forward(0)
 
-    def chain_sum(part, chain, tree, p, counts, streams, rank, finished):
+    def chain_sum(part, chain, tree, p, blocks, counts, streams, rank, finished):
         kind = chain.dtype
         rows = chain.shape[3]
         edges = [0, rows] if streams == 1 else [0, PR, rows]
         left = [2 * streams]
 
         def term(lo, hi, chunk):
-            span = pl.ds(pl.multiple_of(p * HALF + chunk * PR, 16), PR)
             pieces = []
-            if lo < PR:
-                pieces.append(part[0, span, :])
-            if hi > PR:
-                pieces.append(part[1, span, :])
-            if hi > 2 * PR:
+            for i, block in enumerate(blocks):
+                span = pl.ds(pl.multiple_of(block * HALF + chunk * PR, 16), PR)
+                for half in range(2):
+                    if lo <= (2 * i + half) * PR < hi:
+                        pieces.append(part[half, span, :])
+            if hi > 2 * len(blocks) * PR:
                 pieces.append(counts)
             return jnp.concatenate(pieces, axis=0) if len(pieces) > 1 else pieces[0]
 
@@ -361,11 +381,10 @@
     sib_target = helpers[sib]
     top_half = lax.broadcasted_iota(jnp.int32, (8, L), 0) < 4
 
-    def plane_sum(plane, cross, total, p, rank, finished):
-        rows = 2 * PR + (8 if p == 0 and plane.dtype == F32 else 0)
-        tallied = rows > 2 * PR
+    def plane_sum(plane, cross, total, p, pairs, rank, finished):
+        rows = 2 * PR * pairs + (8 if p == 0 and plane.dtype == F32 else 0)
+        tallied = rows > 2 * PR * pairs
         kb = rows * L * (4 if plane.dtype == F32 else 2) / 1000.0
-        lo, hi = pl.ds(0, PR), pl.ds(PR, rows - PR)
         passed = []
         left = [8]
         whole = pl.ds(0, rows)
@@ -382,21 +401,19 @@
         def item(dx, dy, *span):
             return plane.at[(p, rem(y + dy, 4), rem(x + dx, 4), *span)]
 
-        def relay(step, source, span, share):
-            ref = item(*source, span)
-            passed.append(send(ref, ref, around[step], kb * share, path(*step)))
+        passes = {
+            (-1, 0): ((1, 0),),
+            (-1, 1): ((1, 0), (0, -1)),
+            (1, -1): ((-1, 0), (0, 1)),
+            (0, -1): ((0, 1),),
+            (1, 1): ((-1, -1),),
+        }
 
         def arrive(dx, dy, flight):
             yield [flight]
-            source = (-dx, -dy)
-            if dx != 0:
-                relay((dx, 0), source, lo if dx > 0 else hi, 0.5)
-            if dy != 0:
-                relay((0, dy), source, lo if dy > 0 else hi, 0.5)
-            if (dx, dy) == (1, 1):
-                relay((1, 1), source, lo, 0.5)
-            if (dx, dy) == (-1, 1):
-                relay((-1, 1), source, hi, 0.5)
+            for step in passes.get((-dx, -dy), ()):
+                ref = item(-dx, -dy, whole)
+                passed.append(send(ref, ref, around[step], kb, path(*step)))
             left[0] -= 1
             if left[0] == 0:
                 plan.spawn(rank, finish())
@@ -412,42 +429,53 @@
                 w_own = jnp.where(its_target == group, 1.0, 0.0)
                 w_help = jnp.where(helpers[group] == its_target, 1.0, 0.0)
                 share = plane.at[p, b, a]
-                home, helped, *tally = carry
-                first, second = share[0:PR, :].astype(F32), share[PR : 2 * PR, :].astype(F32)
-                home = home + w_home * second
-                helped = helped + w_own * first + w_help * second
+                sums_of, tally = list(carry[: 2 * pairs]), carry[2 * pairs :]
+                for i in range(0, 2 * pairs, 2):
+                    first = share[i * PR : (i + 1) * PR, :].astype(F32)
+                    second = share[(i + 1) * PR : (i + 2) * PR, :].astype(F32)
+                    sums_of[i] = sums_of[i] + w_home * second
+                    sums_of[i + 1] = sums_of[i + 1] + w_own * first + w_help * second
                 if tallied:
                     count = share[2 * PR : rows, :]
-                    tally = [
+                    tally = (
                         tally[0] + w_home * count,
                         tally[1] + w_own * count,
                         tally[2] + w_help * count,
-                    ]
-                return (home, helped, *tally)
+                    )
+                return (*sums_of, *tally)
 
             zero = jnp.zeros((PR, L), F32)
             none = jnp.zeros((8, L), F32)
-            carry = (zero, zero) + ((none,) * 3 if tallied else ())
-            home, helped, *tally = lax.fori_loop(0, 16, step, carry)
-            plan.spend(0.6 / PARTS)
+            carry = (zero,) * (2 * pairs) + ((none,) * 3 if tallied else ())
+            carry = lax.fori_loop(0, 16, step, carry)
+            plan.spend(0.3 * pairs)
+            sums_of, tally = carry[: 2 * pairs], carry[2 * pairs :]
             if tallied:
                 first = jnp.broadcast_to(tally[0][4:5, :], (8, L))
                 second = jnp.broadcast_to(tally[1][0:1, :] + tally[2][4:5, :], (8, L))
-                return home, helped, jnp.where(top_half, first, second)
-            return home, helped, None
+                return sums_of, jnp.where(top_half, first, second)
+            return sums_of, None
 
         def finish():
             yield list(passed)
-            home, helped, tally = sums(sib, sib_target)
-            cross[p, 0, 0:PR, :] = home
-            cross[p, 0, PR : 2 * PR, :] = helped
+            sums_of, tally = sums(sib, sib_target)
+            for i in range(2 * pairs):
+                cross[p, 0, i * PR : (i + 1) * PR, :] = sums_of[i]
             if tallied:
                 cross[p, 0, 2 * PR : rows, :] = tally
-            swap = send(cross.at[p, 0, whole], cross.at[p, 1, whole], other, rows * 0.512, (("core", 1, 1),))
-            home, helped, tally = sums(g, target)
+            swap = send(
+                cross.at[p, 0, whole],
+                cross.at[p, 1, whole],
+                other,
+                rows * 0.512,
+                (("core", 1, 1),),
+            )
+            sums_of, tally = sums(g, target)
             yield [swap]
-            total[p, 0:PR, :] = total[p, 0:PR, :] + home + cross[p, 1, 0:PR, :]
-            total[p, PR : 2 * PR, :] = helped + cross[p, 1, PR : 2 * PR, :]
+            for i in range(2 * pairs):
+                span = slice(i * PR, (i + 1) * PR)
+                here = sums_of[i] + cross[p, 1, span, :]
+                total[p, span, :] = total[p, span, :] + here if i % 2 == 0 else here
             if tallied:
                 own = jnp.where(top_half, total[p, 2 * PR : rows, :], 0.0)
                 total[p, 2 * PR : rows, :] = own + tally + cross[p, 1, 2 * PR : rows, :]
@@ -470,13 +498,6 @@
 
     first_half = (lax.broadcasted_iota(jnp.int32, (1, L), 1) < L // 2).astype(F32)
     halves = (first_half, 1.0 - first_half)
-
-    def norm(row):
-        center = jnp.sum(row, axis=-1, keepdims=True) * (1.0 / D)
-        centred = row - center
-        spread_of = jnp.sum(centred * centred, axis=-1, keepdims=True) * (1.0 / D)
-        rstd = lax.rsqrt(spread_of + 1e-05)
-        return centred * rstd, rstd
 
     def normalise():
         plan.spend(1.2)
@@ -555,7 +576,7 @@
     state = {"sent": 0, "soft": set(), "grad": set(), "probs": 0, "dlog": 0, "applied": False}
     state.update(terms=False, led=False, late=list(range(PARTS)))
     scalings = []
-    put_out = pltpu.make_async_copy(out, out_ref, own_sems.at[6])
+    put_proj = pltpu.make_async_copy(proj, proj_ref, own_sems.at[6])
 
     def share_rows(p):
         return pl.ds(pl.multiple_of(p * HALF + z * PR, 16), PR)
@@ -563,7 +584,7 @@
     def scores_summed(p, total):
         s_tot[p, 0 : total.shape[0], :] = total
         plan.mark(("scores summed", p))
-        plane_sum(s_plane, s_cross, s_tot, p, 1, soften)
+        plane_sum(s_plane, s_cross, s_tot, p, 1, 1, soften)
 
     def grads_summed(p, total):
         g_tot[p] = total
@@ -573,7 +594,8 @@
 
     def release():
         while held and state["sent"] >= HOLD:
-            plane_sum(g_plane, g_cross, g_tot, held.pop(0), 2, grads_known)
+            i = held.pop(0)
+            plane_sum(g_plane, g_cross, g_tot, i, len(G_BLOCKS[i]), 2, grads_known)
 
     def soften(p):
         plan.spend(0.5 / PARTS)
@@ -591,9 +613,16 @@
         spread(probs, Z_TREE, p, 3, probs_here)
         differentiate(p)
 
-    def grads_known(p):
-        state["grad"].add(p)
-        differentiate(p)
+    def grads_known(i):
+        for p in G_BLOCKS[i]:
+            state["grad"].add(p)
+            differentiate(p)
+
+    def grads_of(p, e):
+        for i, blocks in enumerate(G_BLOCKS):
+            if p in blocks:
+                start = (2 * blocks.index(p) + e) * PR
+                return g_tot[i, start : start + PR, :]
 
     def differentiate(p):
         if p not in state["soft"] or p not in state["grad"]:
@@ -602,7 +631,7 @@
         plan.mark(("dlogit", p))
         for e in range(2):
             share = attend[e, p * PR : (p + 1) * PR, :]
-            grads = g_tot[p, e * PR : (e + 1) * PR, :]
+            grads = grads_of(p, e)
             mean = jnp.sum(grads * share, axis=-1, keepdims=True)
             dlog[e, share_rows(p), :] = (share * (grads - mean) * scalings[e]).astype(BF16)
         spread(dlog, Z_TREE, p, 2, dlog_here)
@@ -647,12 +676,9 @@
         @pl.loop(0, 3)
         def _(n):
             cols = pl.ds(pl.multiple_of(n * 256, 256), 256)
-            part = dot(attended[...], weights[3, :, cols])
-            for r in range(RDEV):
-                rows = slice(r * L, (r + 1) * L)
-                out[r, :, cols] = (emb[r, :, cols].astype(F32) + part[rows, :]).astype(BF16)
-
-        put_out.start()
+            proj[:, cols] = dot(attended[...], weights[3, :, cols])
+
+        put_proj.start()
         yield []
         plan.spend(0.8)
 
@@ -682,8 +708,14 @@
     def lead():
         if state["terms"] and steps[0] >= S_LEAD and not state["led"]:
             state["led"] = True
-            for p in range(PARTS):
-                chain_sum(g_part, g_chain, G_TREE, p, None, G_STREAMS, 2, grads_summed)
+            for i, blocks in enumerate(G_BLOCKS):
+                chain_sum(
+                    g_part, g_chain, G_TREE, i, blocks, None, G_STREAMS, 2, grads_summed
+                )
+
+    def put_grad(n):
+        cols = pl.ds(pl.multiple_of(n * 256, 256), 256)
+        return pltpu.make_async_copy(dnormed.at[:, cols], grad_ref.at[:, cols], own_sems.at[7 + n])
 
     plan.spend(3.0)
     weight_set(0, 0)
@@ -697,7 +729,7 @@
         project(1, keys, p)
         pair_terms(queries, keys, home_live, help_live, s_part, False, p * PP, p * PP + PP)
         chain = s_chain.at[:, :, :, 0 : 2 * PR + (8 if p == 0 else 0)]
-        chain_sum(s_part, chain, S_TREE, p, counts, S_STREAMS, 1, scores_summed)
+        chain_sum(s_part, chain, S_TREE, p, (p,), counts, S_STREAMS, 1, scores_summed)
     plan.run(lambda: arrived[1] == 8)
     plan.mark("weights 1")
     plan.spawn(9, grad_terms())
@@ -717,38 +749,27 @@
         dnormed[:, cols] += dot_t(dquery[...], weights[0, cols, :]) + dot_t(
             dkey[...], weights[1, cols, :]
         )
-
-    @pl.loop(0, RDEV)
-    def _(r):
-        rows = pl.ds(pl.multiple_of(r * L, L), L)
-        unit, rstd = norm(emb[r].astype(F32))
-        grad = dnormed[rows, :]
-        mean = jnp.sum(grad, axis=-1, keepdims=True) * (1.0 / D)
-        along = jnp.sum(grad * unit, axis=-1, keepdims=True) * (1.0 / D)
-        back = rstd * (grad - mean - unit * along)
-        gin[r] = (cot[r].astype(F32) + back).astype(BF16)
-        pltpu.make_async_copy(gin.at[r], gin_ref.at[r], own_sems.at[7 + r]).start()
+        put_grad(n).start()
 
     for flight in plan.out:
         flight.copy.wait_send()
-    put_out.wait()
-    for r in range(RDEV):
-        pltpu.make_async_copy(gin.at[r], gin_ref.at[r], own_sems.at[7 + r]).wait()
+    put_proj.wait()
+    for n in range(3):
+        put_grad(n).wait()
 
 
 def per_device(*args):
     rows = RDEV * L
     hbm = pl.BlockSpec(memory_space=pl.ANY)
     smem = pl.BlockSpec(memory_space=pltpu.SMEM)
-    shape = jax.ShapeDtypeStruct((RDEV, L, D), BF16)
+    wide = jax.ShapeDtypeStruct((rows, D), F32)
     flat = pltpu.VMEM((rows, D), BF16)
     block = pltpu.VMEM((RDEV, L, D), BF16)
-    s_rows, g_rows = 2 * PR + 8, 2 * PR
+    s_rows, g_rows = 2 * PR + 8, 2 * PR * len(G_BLOCKS[0])
     scratch = [
         block,
         block,
-        block,
-        block,
+        pltpu.VMEM((rows, D), F32),
         pltpu.VMEM((4, D, D), BF16),
         flat,
         flat,
@@ -758,13 +779,13 @@
         pltpu.VMEM((2, HEADS * L, L), F32),
         pltpu.VMEM((2, HEADS * L, L), F32),
         pltpu.VMEM((PARTS, 2, 16, s_rows, L), F32),
-        pltpu.VMEM((PARTS, 2, 16, g_rows, L), BF16),
+        pltpu.VMEM((len(G_BLOCKS), 2, 16, g_rows, L), BF16),
         pltpu.VMEM((PARTS, 4, 4, s_rows, L), F32),
-        pltpu.VMEM((PARTS, 4, 4, g_rows, L), BF16),
+        pltpu.VMEM((len(G_BLOCKS), 4, 4, g_rows, L), BF16),
         pltpu.VMEM((PARTS, 2, s_rows, L), F32),
-        pltpu.VMEM((PARTS, 2, g_rows, L), F32),
+        pltpu.VMEM((len(G_BLOCKS), 2, g_rows, L), F32),
         pltpu.VMEM((PARTS, s_rows, L), F32),
-        pltpu.VMEM((PARTS, g_rows, L), F32),
+        pltpu.VMEM((len(G_BLOCKS), g_rows, L), F32),
         pltpu.VMEM((2, CH, L), F32),
         pltpu.VMEM((2, HEADS * L, L), BF16),
         pltpu.VMEM((2, HEADS * L, L), BF16),
@@ -775,18 +796,29 @@
         pltpu.VMEM((rows, D), F32),
         pltpu.SemaphoreType.DMA((N_SEM,)),
         pltpu.SemaphoreType.DMA((N_SEM,)),
-        pltpu.SemaphoreType.DMA((11,)),
+        pltpu.SemaphoreType.DMA((10,)),
     ]
-    return pl.pallas_call(
+    proj, grads = pl.pallas_call(
         kernel,
-        out_shape=(shape, shape),
+        out_shape=(wide, wide),
         in_specs=[hbm] * 6 + [smem] * 3,
         out_specs=(hbm, hbm),
         scratch_shapes=scratch,
         compiler_params=pltpu.CompilerParams(
-            collective_id=0, has_side_effects=True, vmem_limit_bytes=56 * 1024 * 1024
+            collective_id=0, has_side_effects=True, vmem_limit_bytes=48 * 1024 * 1024
         ),
     )(*args)
+    shape = jax.ShapeDtypeStruct((RDEV, L, D), BF16)
+    row = pl.BlockSpec((1, L, D), lambda r: (r, 0, 0))
+    flat_row = pl.BlockSpec((L, D), lambda r: (r, 0))
+    return pl.pallas_call(
+        finish_rows,
+        grid=(RDEV,),
+        out_shape=(shape, shape),
+        in_specs=[row, row, flat_row, flat_row],
+        out_specs=(row, row),
+        compiler_params=pltpu.CompilerParams(vmem_limit_bytes=16 * 1024 * 1024),
+    )(args[0], args[1], proj, grads)
 
 
 def solution(mesh):

time: 127 us -> 131 us (1.031)
  local copies, waits for them, and re-layouts: 3.02 us -> 7.76 us
    unnamed x4 -> x18, local copies, waits for them, and re-layouts: 3.02 us -> 7.76 us
    pallas_call x1 -> x2, Pallas kernels: 122 us -> 121 us  [the longest x1 119 us: per_device(): pl.pallas_call(kernel, out_shape=(wide, wide), in_specs=[hbm] * 6 + [smem...]
where the time goes in v3:
time: 131 us; the launch traced here: 129 us
  Pallas kernels  121 us (92%)
  local copies, waits for them, and re-layouts  7.76 us (6%)
    pallas_call x1, Pallas kernels, per_device(): pl.pallas_call(kernel, out_shape=(wide, wide), in_specs=[hbm] * 6 + [smem...  119 us
    unnamed x18, local copies, waits for them, and re-layouts  7.76 us

profile of v3, /device:TPU:6, one launch (start us, length us, event | category | flops | bytes accessed | tf_op | source)
XLA Modules:
  0.0 129.5 jit_solution(10494398652717966672)
XLA Ops:
  0.6 0.0 copy-start
  0.6 1.1 copy-done
  1.8 0.0 copy-start.1
  1.8 1.1 copy-done.1
  2.9 0.0 copy-start.2
  2.9 0.9 copy-done.2
  3.8 0.0 copy-start.3
  3.8 0.9 copy-done.3
  4.7 0.0 copy-start.4
  4.7 0.9 copy-done.4
  5.6 0.0 copy-start.5
  5.6 0.9 copy-done.5
  6.4 0.0 copy-start.6
  6.4 0.7 copy-done.6
  7.1 0.0 copy-start.7
  7.1 0.7 copy-done.7
  7.8 0.0 copy-start.8
  7.8 0.7 copy-done.8
  8.4 118.6 %shard_map.104 = (f32[512,768]{1,0:T(8,128)S(1)}, f32[512,768]{1,0:T(8,128)S(1)}) custom-call(bf16[4,128,768]{2,1,0:T(8,128)(2,1)S(1)} %copy-done, bf16[4,128,768]{2,1,0:T(8,128)(2,1)S(1)} %copy-done.1, bf16[48,768]{1,0:T(8,128)(2,1)S(1)} %copy-done.2, bf16[48,768]{1,0:T(8,128)(2,1)S(1)} %copy-done.3, bf16[48,768]{1,0:T(8,128)(2,1)S(1)} %copy-done.4, ...), custom_call_target="tpu_custom_call" | custom-call | tf_op jit(solution)/shard_map/pallas_call | solution.py:801
  127.1 2.4 %shard_map.105 = (bf16[4,128,768]{2,1,0:T(8,128)(2,1)}, bf16[4,128,768]{2,1,0:T(8,128)(2,1)}) custom-call(bf16[4,128,768]{2,1,0:T(8,128)(2,1)S(1)} %copy-done, bf16[4,128,768]{2,1,0:T(8,128)(2,1)S(1)} %copy-done.1, f32[512,768]{1,0:T(8,128)S(1)} %get-tuple-element.4.proj, f32[512,768]{1,0:T(8,128)S(1)} %get-tuple-element.5.grads), custom_call_target="tpu_custom_call" | custom-call | tf_op jit(solution)/shard_map/pallas_call | solution.py:814
Async XLA Ops:
  0.6 1.1 copy-start
  1.8 1.1 copy-start.1
  2.9 0.9 copy-start.2
  3.8 0.9 copy-start.3
  4.7 0.9 copy-start.4
  5.6 0.9 copy-start.5
  6.4 0.7 copy-start.6
  7.1 0.7 copy-start.7
  7.8 0.7 copy-start.8

commit v4 on v3

--- a/solution.py
+++ b/solution.py
@@ -805,7 +805,7 @@
         out_specs=(hbm, hbm),
         scratch_shapes=scratch,
         compiler_params=pltpu.CompilerParams(
-            collective_id=0, has_side_effects=True, vmem_limit_bytes=48 * 1024 * 1024
+            collective_id=0, has_side_effects=True, vmem_limit_bytes=60 * 1024 * 1024
         ),
     )(*args)
     shape = jax.ShapeDtypeStruct((RDEV, L, D), BF16)
@@ -817,7 +817,7 @@
         out_shape=(shape, shape),
         in_specs=[row, row, flat_row, flat_row],
         out_specs=(row, row),
-        compiler_params=pltpu.CompilerParams(vmem_limit_bytes=16 * 1024 * 1024),
+        compiler_params=pltpu.CompilerParams(vmem_limit_bytes=60 * 1024 * 1024),
     )(args[0], args[1], proj, grads)
 
 

time: 131 us -> 126 us (0.962)
  local copies, waits for them, and re-layouts: 7.76 us -> 0 us
  Pallas kernels: 121 us -> 124 us
    unnamed x18 -> x0, local copies, waits for them, and re-layouts: 7.76 us -> none
    pallas_call x1, Pallas kernels: 2.42 us -> 4.68 us  [per_device(): pl.pallas_call(finish_rows, grid=(RDEV,), out_shape=(shape, shape), in_sp...]
where the time goes in v4:
time: 126 us; the launch traced here: 125 us
  Pallas kernels  124 us (98%)
    pallas_call x1, Pallas kernels, per_device(): pl.pallas_call(kernel, out_shape=(wide, wide), in_specs=[hbm] * 6 + [smem...  120 us
    pallas_call x1, Pallas kernels, per_device(): pl.pallas_call(finish_rows, grid=(RDEV,), out_shape=(shape, shape), in_sp...  4.68 us

profile of v4, /device:TPU:6, one launch (start us, length us, event | category | flops | bytes accessed | tf_op | source)
XLA Modules:
  0.0 125.0 jit_solution(9274138067885490159)
XLA Ops:
  0.6 119.6 %shard_map.104 = (f32[512,768]{1,0:T(8,128)}, f32[512,768]{1,0:T(8,128)}) custom-call(bf16[4,128,768]{2,1,0:T(8,128)(2,1)} %emb.1, bf16[4,128,768]{2,1,0:T(8,128)(2,1)} %cot.1, bf16[48,768]{1,0:T(8,128)(2,1)} %w_query.1, bf16[48,768]{1,0:T(8,128)(2,1)} %w_key.1, bf16[48,768]{1,0:T(8,128)(2,1)} %w_value.1, bf16[48,768]{1,0:T(8,128)(2,1)} %w_output.1, ...), custom_call_target="tpu_custom_call" | custom-call | tf_op jit(solution)/shard_map/pallas_call | solution.py:801
  120.3 4.7 %shard_map.105 = (bf16[4,128,768]{2,1,0:T(8,128)(2,1)}, bf16[4,128,768]{2,1,0:T(8,128)(2,1)}) custom-call(bf16[4,128,768]{2,1,0:T(8,128)(2,1)} %emb.1, bf16[4,128,768]{2,1,0:T(8,128)(2,1)} %cot.1, f32[512,768]{1,0:T(8,128)} %get-tuple-element.4.proj, f32[512,768]{1,0:T(8,128)} %get-tuple-element.5.grads), custom_call_target="tpu_custom_call" | custom-call | tf_op jit(solution)/shard_map/pallas_call | solution.py:814

commit v5 on v4

--- a/solution.py
+++ b/solution.py
@@ -131,16 +131,6 @@
     return centred * rstd, rstd
 
 
-def finish_rows(emb, cot, proj, grads, out, gin):
-    row = emb[0].astype(F32)
-    out[0] = (row + proj[...]).astype(BF16)
-    unit, rstd = norm(row)
-    grad = grads[...]
-    mean = jnp.sum(grad, axis=-1, keepdims=True) * (1.0 / D)
-    along = jnp.sum(grad * unit, axis=-1, keepdims=True) * (1.0 / D)
-    gin[0] = (cot[0].astype(F32) + rstd * (grad - mean - unit * along)).astype(BF16)
-
-
 def kernel(
     emb_in,
     cot_in,
@@ -152,10 +142,13 @@
     flag,
     live,
     proj_ref,
-    grad_ref,
+    gin_ref,
     emb,
     cot,
     proj,
+    gin,
+    unit,
+    scale_in,
     weights,
     normed,
     queries,
@@ -505,7 +498,10 @@
         @pl.loop(0, RDEV)
         def _(r):
             rows = pl.ds(pl.multiple_of(r * L, L), L)
-            normed[rows, :] = norm(emb[r].astype(F32))[0].astype(BF16)
+            here, rstd = norm(emb[r].astype(F32))
+            unit[rows, :] = here
+            scale_in[rows, :] = jnp.broadcast_to(rstd, (L, L))
+            normed[rows, :] = here.astype(BF16)
 
     def project(m, dst, p):
         plan.spend(0.5)
@@ -712,10 +708,6 @@
                 chain_sum(
                     g_part, g_chain, G_TREE, i, blocks, None, G_STREAMS, 2, grads_summed
                 )
-
-    def put_grad(n):
-        cols = pl.ds(pl.multiple_of(n * 256, 256), 256)
-        return pltpu.make_async_copy(dnormed.at[:, cols], grad_ref.at[:, cols], own_sems.at[7 + n])
 
     plan.spend(3.0)
     weight_set(0, 0)
@@ -749,13 +741,22 @@
         dnormed[:, cols] += dot_t(dquery[...], weights[0, cols, :]) + dot_t(
             dkey[...], weights[1, cols, :]
         )
-        put_grad(n).start()
+
+    @pl.loop(0, RDEV)
+    def _(r):
+        rows = pl.ds(pl.multiple_of(r * L, L), L)
+        grad, here = dnormed[rows, :], unit[rows, :]
+        mean = jnp.sum(grad, axis=-1, keepdims=True) * (1.0 / D)
+        along = jnp.sum(grad * here, axis=-1, keepdims=True) * (1.0 / D)
+        back = scale_in[rows, 0:1] * (grad - mean - here * along)
+        gin[r] = (cot[r].astype(F32) + back).astype(BF16)
+        pltpu.make_async_copy(gin.at[r], gin_ref.at[r], own_sems.at[7 + r]).start()
 
     for flight in plan.out:
         flight.copy.wait_send()
     put_proj.wait()
-    for n in range(3):
-        put_grad(n).wait()
+    for r in range(RDEV):
+        pltpu.make_async_copy(gin.at[r], gin_ref.at[r], own_sems.at[7 + r]).wait()
 
 
 def per_device(*args):
@@ -763,6 +764,7 @@
     hbm = pl.BlockSpec(memory_space=pl.ANY)
     smem = pl.BlockSpec(memory_space=pltpu.SMEM)
     wide = jax.ShapeDtypeStruct((rows, D), F32)
+    shape = jax.ShapeDtypeStruct((RDEV, L, D), BF16)
     flat = pltpu.VMEM((rows, D), BF16)
     block = pltpu.VMEM((RDEV, L, D), BF16)
     s_rows, g_rows = 2 * PR + 8, 2 * PR * len(G_BLOCKS[0])
@@ -770,6 +772,9 @@
         block,
         block,
         pltpu.VMEM((rows, D), F32),
+        block,
+        pltpu.VMEM((rows, D), F32),
+        pltpu.VMEM((rows, L), F32),
         pltpu.VMEM((4, D, D), BF16),
         flat,
         flat,
@@ -796,11 +801,11 @@
         pltpu.VMEM((rows, D), F32),
         pltpu.SemaphoreType.DMA((N_SEM,)),
         pltpu.SemaphoreType.DMA((N_SEM,)),
-        pltpu.SemaphoreType.DMA((10,)),
+        pltpu.SemaphoreType.DMA((11,)),
     ]
-    proj, grads = pl.pallas_call(
+    proj, gin = pl.pallas_call(
         kernel,
-        out_shape=(wide, wide),
+        out_shape=(wide, shape),
         in_specs=[hbm] * 6 + [smem] * 3,
         out_specs=(hbm, hbm),
         scratch_shapes=scratch,
@@ -808,17 +813,8 @@
             collective_id=0, has_side_effects=True, vmem_limit_bytes=60 * 1024 * 1024
         ),
     )(*args)
-    shape = jax.ShapeDtypeStruct((RDEV, L, D), BF16)
-    row = pl.BlockSpec((1, L, D), lambda r: (r, 0, 0))
-    flat_row = pl.BlockSpec((L, D), lambda r: (r, 0))
-    return pl.pallas_call(
-        finish_rows,
-        grid=(RDEV,),
-        out_shape=(shape, shape),
-        in_specs=[row, row, flat_row, flat_row],
-        out_specs=(row, row),
-        compiler_params=pltpu.CompilerParams(vmem_limit_bytes=60 * 1024 * 1024),
-    )(args[0], args[1], proj, grads)
+    out = (args[0].astype(F32) + proj.reshape(RDEV, L, D)).astype(BF16)
+    return out, gin
 
 
 def solution(mesh):

time: 126 us -> 126 us (level)
  Pallas kernels: 124 us -> 120 us
  other arithmetic: 0 us -> 2.52 us
    pallas_call x2 -> x1, Pallas kernels: 124 us -> 120 us  [per_device(): pl.pallas_call(kernel, out_shape=(wide, shape), in_specs=[hbm] * 6 + [sme...]
    convert_element_type x0 -> x1, other arithmetic: none -> 2.52 us  [per_device(): out = (args[0].astype(F32) + proj.reshape(RDEV, L, D)).astype(BF16)]
where the time goes in v5:
time: 126 us; the launch traced here: 124 us
  Pallas kernels  120 us (95%)
  other arithmetic  2.52 us (2%)
    pallas_call x1, Pallas kernels, per_device(): pl.pallas_call(kernel, out_shape=(wide, shape), in_specs=[hbm] * 6 + [sme...  120 us

profile of v5, /device:TPU:6, one launch (start us, length us, event | category | flops | bytes accessed | tf_op | source)
XLA Modules:
  0.0 124.3 jit_solution(918891694289232815)
XLA Ops:
  0.6 0.0 copy-start
  0.6 120.3 %shard_map.104 = (f32[512,768]{1,0:T(8,128)}, bf16[4,128,768]{2,1,0:T(8,128)(2,1)}) custom-call(bf16[4,128,768]{2,1,0:T(8,128)(2,1)} %emb_in.1, bf16[4,128,768]{2,1,0:T(8,128)(2,1)} %cot_in.1, bf16[48,768]{1,0:T(8,128)(2,1)} %w_query.1, bf16[48,768]{1,0:T(8,128)(2,1)} %w_key.1, bf16[48,768]{1,0:T(8,128)(2,1)} %w_value.1, bf16[48,768]{1,0:T(8,128)(2,1)} %w_output.1, ...), custom_call_target="tpu_custom_call" | custom-call | tf_op jit(solution)/shard_map/pallas_call | solution.py:806
  120.9 0.0 copy-done
  120.9 0.0 copy-start.1
  120.9 2.5 %add_convert_fusion = bf16[4,128,768]{2,1,0:T(8,128)(2,1)} fusion(f32[4,128,768]{2,1,0:T(8,128)} %bitcast.1, bf16[4,128,768]{2,1,0:T(8,128)(2,1)S(1)} %copy-done), kind=kLoop, calls=%fused_computation | loop fusion | flops 1179648 | bytes 3145728 | tf_op jit(solution)/shard_map/convert_element_type | solution.py:816
  123.5 0.0 copy-done.1
  123.5 0.9 copy.12
Async XLA Ops:
  0.6 120.3 %copy-start = (bf16[4,128,768]{2,1,0:T(8,128)(2,1)S(1)}, bf16[4,128,768]{2,1,0:T(8,128)(2,1)}, u32[]{:S(2)}) copy-start(bf16[4,128,768]{2,1,0:T(8,128)(2,1)} %emb_in.1) | copy-start | bytes 2359300
  120.9 2.5 %copy-start.1 = (bf16[4,128,768]{2,1,0:T(8,128)(2,1)S(1)}, bf16[4,128,768]{2,1,0:T(8,128)(2,1)}, u32[]{:S(2)}) copy-start(bf16[4,128,768]{2,1,0:T(8,128)(2,1)} %get-tuple-element.9) | copy-start | bytes 2359300
